TPU v7x, 32 devices: a whole 2x2x4 slice. The times are simulated.
32 devices in a mesh: role: 2 (over x), dp: 2 (over core), hidden: 8 (over z, y).
Axes of the slice: x: 2, y: 2, z: 4, core: 2. Of those that a mesh axis runs over, the one named last changes fastest.
Arguments:
- token_rows: bfloat16 [2, 256, 5120], P('role', 'dp'), may hold values from -6 to 6
- cotangent: bfloat16 [256, 5120], P('dp'), may hold values from -6 to 6
- staleness: int32 [256], P('dp'), may hold values from 0 to 7
- prefill_rows: int32 [2], P('dp'), may hold values from 1 to 128, as said below
- frozen_gate_up_weight: bfloat16 [2, 5120, 13824], P(None, ('role', 'dp'), 'hidden'), may hold values from -0.078125 to 0.078125
- down_weight: bfloat16 [13824, 5120], P('hidden', ('role', 'dp')), may hold values from -0.0546875 to 0.0546875
- adapter_in: float32 [2, 5120, 32], P(None, 'hidden'), may hold values from -0.078125 to 0.078125
- adapter_out: float32 [2, 32, 13824], P(None, None, 'hidden'), may hold values from -0.6 to 0.6
- moment_in: float32 [2, 5120, 32], P(None, 'hidden'), may hold values from -274.76804 to 274.76804
- square_in: float32 [2, 5120, 32], P(None, 'hidden'), may hold values from 5.24288 to 524.288
- moment_out: float32 [2, 32, 13824], P(None, None, 'hidden'), may hold values from -1.2 to 1.2
- square_out: float32 [2, 32, 13824], P(None, None, 'hidden'), may hold values from 0.01 to 1
Outputs:
- layer_old: bfloat16 [2, 256, 5120], P('role', 'dp', 'hidden')
- layer_new: bfloat16 [2, 256, 5120], P('role', 'dp', 'hidden')
- new_adapter_in: float32 [2, 2, 5120, 32], P('role', None, 'hidden')
- new_adapter_out: float32 [2, 2, 32, 13824], P('role', None, None, 'hidden')
- new_moment_in: float32 [2, 2, 5120, 32], P('role', None, 'hidden')
- new_square_in: float32 [2, 2, 5120, 32], P('role', None, 'hidden')
- new_moment_out: float32 [2, 2, 32, 13824], P('role', None, None, 'hidden')
- new_square_out: float32 [2, 2, 32, 13824], P('role', None, None, 'hidden')
Inputs may be any that keep to these rules, and one draw needn't show every extreme that they name: The first prefill_rows[g] rows of rollout group g are live, the rest are padding; some group is full in every draw.
All inputs are finite; a program needn't handle non-finite values.
Results may differ from a plain program's by a relative error of at most 0.025.
Values may be sent and summed in bfloat16 or wider, within the bound.
A program may use at most 128 MiB of HBM per device.

v0:
```python
import jax
import jax.numpy as jnp
from jax import lax
from jax.sharding import PartitionSpec as P

D = 5120
OPT_STEP = 10


ADAPTER_SCALE = 2.0
BETA_ONE = 0.9
BETA_TWO = 0.999
RATE_FACTOR = 0.34
ADAM_EPS = 1e-08
KEEP_RATE = 0.75


def from_behind(value, axis, steps):
    count = lax.axis_size(axis)
    first, last = (max(0, -steps), min(count, count - steps))
    return lax.ppermute(value, axis, [(source, source + steps) for source in range(first, last)])


def adam_update(param, grad, first, second):
    learn_rate = RATE_FACTOR / D**0.5
    first_new = BETA_ONE * first + (1.0 - BETA_ONE) * grad
    second_new = BETA_TWO * second + (1.0 - BETA_TWO) * grad * grad
    first_fix = first_new / (1.0 - BETA_ONE**OPT_STEP)
    second_fix = second_new / (1.0 - BETA_TWO**OPT_STEP)
    return (
        param - learn_rate * first_fix / (jnp.sqrt(second_fix) + ADAM_EPS),
        first_new,
        second_new,
    )


def finish(hidden_act, full_down, live):
    partial_value = jnp.dot(hidden_act, full_down, preferred_element_type=jnp.float32)
    summed = lax.psum_scatter(
        partial_value.astype(jnp.bfloat16), "hidden", scatter_dimension=1, tiled=True
    )
    return jnp.where(live[:, None], summed, jnp.zeros_like(summed))


def local(
    token_rows,
    cotangent,
    staleness,
    prefill_rows,
    frozen_gate_up_weight,
    down_weight,
    adapter_in,
    adapter_out,
    moment_in,
    square_in,
    moment_out,
    square_out,
):
    half_index = lax.axis_index("role")
    shard_index = lax.axis_index("hidden")
    token_batch = token_rows[0]
    group_rows = token_batch.shape[0]
    slice_width = adapter_in.shape[1]
    hidden_cols = frozen_gate_up_weight.shape[2]
    token_part = lax.dynamic_slice_in_dim(token_batch, shard_index * slice_width, slice_width, 1)
    piece = lax.all_gather(frozen_gate_up_weight, ("role", "dp"), axis=1, tiled=True)
    base_sum = jnp.einsum("rd,kdf->krf", token_batch, piece, preferred_element_type=jnp.float32)
    full_down = lax.all_gather(down_weight, ("role", "dp"), axis=1, tiled=True)
    reduced_part = jnp.einsum(
        "rd,kdq->krq",
        token_part,
        adapter_in.astype(jnp.bfloat16),
        preferred_element_type=jnp.float32,
    )
    reduced_gradient = lax.psum(reduced_part, "hidden").astype(jnp.bfloat16)
    out_bf = adapter_out.astype(jnp.bfloat16)
    lifted_rows = jnp.einsum(
        "krq,kqf->krf", reduced_gradient, out_bf, preferred_element_type=jnp.float32
    )
    stale_preactivation = base_sum + ADAPTER_SCALE * lifted_rows
    hidden_old = (jax.nn.silu(stale_preactivation[0]) * stale_preactivation[1]).astype(jnp.bfloat16)
    positions = jnp.arange(group_rows)
    live = jnp.logical_or(half_index == 0, positions < prefill_rows[0])
    layer_old = finish(hidden_old, full_down, live)
    row_weight = KEEP_RATE ** staleness.astype(jnp.float32)
    upstream = (row_weight[:, None] * cotangent.astype(jnp.float32)).astype(jnp.bfloat16)
    grad_hidden = lax.cond(
        half_index == 0,
        lambda: lax.dot_general(
            upstream, full_down, (((1,), (1,)), ((), ())), preferred_element_type=jnp.float32
        ),
        lambda: jnp.zeros((group_rows, hidden_cols), jnp.float32),
    )
    sigma = jax.nn.sigmoid(stale_preactivation[0])
    grad_gate = (
        grad_hidden
        * stale_preactivation[1]
        * sigma
        * (1.0 + stale_preactivation[0] * (1.0 - sigma))
    ).astype(jnp.bfloat16)
    grad_up = (grad_hidden * stale_preactivation[0] * sigma).astype(jnp.bfloat16)
    gradient_tree = jnp.stack([grad_gate, grad_up])
    partial_out_gradient = ADAPTER_SCALE * jnp.einsum(
        "aod,aot->adt", reduced_gradient, gradient_tree, preferred_element_type=jnp.float32
    )
    through_part = jnp.einsum(
        "krf,kqf->krq", gradient_tree, out_bf, preferred_element_type=jnp.float32
    )
    passed_through = lax.psum(through_part, "hidden").astype(jnp.bfloat16)
    partial_in_gradient = ADAPTER_SCALE * jnp.einsum(
        "un,huj->hnj", token_part, passed_through, preferred_element_type=jnp.float32
    )
    adapter_in_gradient, adapter_out_gradient = lax.psum(
        (partial_in_gradient, partial_out_gradient), "dp"
    )
    own_in, own_m_in, own_s_in = adam_update(adapter_in, adapter_in_gradient, moment_in, square_in)
    own_out, own_m_out, own_s_out = adam_update(
        adapter_out, adapter_out_gradient, moment_out, square_out
    )
    sent = from_behind((own_in, own_out, own_m_in, own_s_in, own_m_out, own_s_out), "role", 1)
    owned = (own_in, own_out, own_m_in, own_s_in, own_m_out, own_s_out)
    picked = jax.tree.map(
        lambda mine, theirs: jnp.where(half_index == 1, theirs, mine), owned, tuple(sent)
    )
    new_in, new_out, new_m_in, new_s_in, new_m_out, new_s_out = picked
    full_in = lax.all_gather(new_in.astype(jnp.bfloat16), "hidden", axis=1, tiled=True)
    updated_out_brainfloat = new_out.astype(jnp.bfloat16)
    post_list = []
    for group_member in range(2):
        merged_weight = (
            piece[group_member].astype(jnp.float32)
            + ADAPTER_SCALE
            * jnp.dot(
                full_in[group_member],
                updated_out_brainfloat[group_member],
                preferred_element_type=jnp.float32,
            )
        ).astype(jnp.bfloat16)
        post_list.append(jnp.dot(token_batch, merged_weight, preferred_element_type=jnp.float32))
    hidden_new = (jax.nn.silu(post_list[0]) * post_list[1]).astype(jnp.bfloat16)
    layer_new = finish(hidden_new, full_down, live)
    return (
        layer_old[None],
        layer_new[None],
        new_in[None],
        new_out[None],
        new_m_in[None],
        new_s_in[None],
        new_m_out[None],
        new_s_out[None],
    )


def solution(mesh):
    in_specs = (
        P("role", "dp", None),
        P("dp", None),
        P("dp"),
        P("dp"),
        P(None, ("role", "dp"), "hidden"),
        P("hidden", ("role", "dp")),
        P(None, "hidden", None),
        P(None, None, "hidden"),
        P(None, "hidden", None),
        P(None, "hidden", None),
        P(None, None, "hidden"),
        P(None, None, "hidden"),
    )
    out_specs = (
        P("role", "dp", "hidden"),
        P("role", "dp", "hidden"),
        P("role", None, "hidden", None),
        P("role", None, None, "hidden"),
        P("role", None, "hidden", None),
        P("role", None, "hidden", None),
        P("role", None, None, "hidden"),
        P("role", None, None, "hidden"),
    )
    return jax.shard_map(local, mesh=mesh, in_specs=in_specs, out_specs=out_specs, check_vma=False)
```

profile of v0, /device:TPU:1, one launch (start us, length us, event | category | flops | bytes accessed | tf_op | source)
XLA Modules:
  0.0 569.0 jit_solution(14886297925232021356)
XLA Ops:
  7.2 0.7 all-gather.5.cloned.1.call-update
  8.0 0.7 all-gather.3.cloned.1.call-update
  8.7 0.1 copy-done.10
  8.9 0.2 fusion.22
  9.1 31.1 %psum.28 = bf16[2,128,32]{1,2,0:T(8,128)(2,1)S(1)} all-reduce(f32[2,128,32]{1,2,0:T(8,128)S(1)} %bitcast.133), channel_id=1, replica_groups=mesh['role'=2,'dp'=2,'hidden'=8] {'hidden'}, use_global_device_ids=true, to_apply=%region_0.0 | all-reduce | flops 8192 | bytes 49152 | tf_op jit(solution)/shard_map/psum | solution.py:75
  40.2 1.7 multiply_convert_fusion
  41.9 83.7 %all-gather.5.cloned.1.call-done = bf16[1728,5120]{1,0:T(8,128)(2,1)} async-done(((bf16[1728,1280]{1,0:T(8,128)(2,1)}), bf16[1728,5120]{1,0:T(8,128)(2,1)}) %all-gather.5.cloned.1.call-update) | async-done | bytes 17694736 | tf_op jit(solution)/shard_map/all_gather | solution.py:68
  125.6 8.5 %conditional.1 = (f32[128,1728]{0,1:T(8,128)S(1)}) conditional(s32[]{:T(128)} %convert_element_type.73, () %tuple.14, (bf16[128,5120]{1,0:T(8,128)(2,1)S(1)}, bf16[1728,5120]{1,0:T(8,128)(2,1)}) %tuple.15), branch_computations={%region_2.3_spmd, %region_3.4_spmd} | conditional | flops 2264924160 | bytes 19890184 | solution.py:87
  125.6 8.5 %fusion.42 = f32[128,1728]{0,1:T(8,128)S(1)} fusion(bf16[128,5120]{1,0:T(8,128)(2,1)S(1)} %get-tuple-element.4, bf16[1728,5120]{1,0:T(8,128)(2,1)} %get-tuple-element.8), kind=kOutput, calls=%fused_computation.78 | convolution fusion | flops 2264924160 | bytes 19890176 | tf_op jit(solution)/shard_map/cond/branch_1_fun/dot_general | solution.py:89
  134.1 207.2 %all-gather.3.cloned.1.call-done = bf16[2,5120,1728]{1,2,0:T(8,128)(2,1)} async-done(((bf16[2,1280,1728]{1,2,0:T(8,128)(2,1)}), bf16[2,5120,1728]{1,2,0:T(8,128)(2,1)}) %all-gather.3.cloned.1.call-update) | async-done | bytes 35389456 | tf_op jit(solution)/shard_map/all_gather | solution.py:66
  341.3 15.3 %convolution_bitcast_fusion = f32[2,128,1728]{1,2,0:T(8,128)S(1)} fusion(bf16[2,5120,1728]{1,2,0:T(8,128)(2,1)} %all-gather.3.cloned.1.call-done, bf16[1,128,5120]{2,1,0:T(8,128)(2,1)S(1)} %copy-done), kind=kOutput, calls=%fused_computation.12 | convolution fusion | flops 4529848320 | bytes 38469632 | tf_op jit(solution)/shard_map/rd,kdf->krf/dot_general | solution.py:67
  356.7 0.5 fusion.4
  357.1 0.7 copy-done.2
  357.8 0.5 fusion.17
  358.3 0.3 fusion.13
  358.6 1.2 convolution_multiply_fusion.1
  359.8 29.9 %psum.29 = bf16[2,128,32]{1,2,0:T(8,128)(2,1)S(1)} all-reduce(f32[2,128,32]{1,2,0:T(8,128)S(1)} %fusion.13), channel_id=1, replica_groups=mesh['role'=2,'dp'=2,'hidden'=8] {'hidden'}, use_global_device_ids=true, to_apply=%region_4.5 | all-reduce | flops 8192 | bytes 49152 | tf_op jit(solution)/shard_map/psum | solution.py:109
  389.6 0.8 fusion.12
  390.5 9.8 %convolution_convert_fusion.1 = bf16[128,5120]{1,0:T(8,128)(2,1)} fusion(bf16[1728,5120]{1,0:T(8,128)(2,1)} %all-gather.5.cloned.1.call-done, f32[2,128,1728]{1,2,0:T(8,128)S(1)} %fusion.4), kind=kOutput, calls=%fused_computation.9 | convolution fusion | flops 2266906624 | bytes 20774912 | tf_op jit(solution)/shard_map/dot_general | solution.py:38
  400.3 2.6 copy.20
  403.0 10.1 %all-reduce.3.cloned.1.call-done = (f32[2,640,32]{1,2,0:T(8,128)}, f32[2,32,1728]{2,1,0:T(8,128)}) async-done(((f32[2,640,32]{1,2,0:T(8,128)}, f32[2,32,1728]{2,1,0:T(8,128)}), (f32[2,640,32]{1,2,0:T(8,128)}, f32[2,32,1728]{2,1,0:T(8,128)})) %all-reduce.3.cloned.1.call-update) | async-done | bytes 606224 | tf_op jit(solution)/shard_map/psum | solution.py:113
  413.1 1.7 divide_subtract_fusion.1
  414.9 3.4 collective-permute-start
  418.3 2.2 divide_subtract_fusion
  420.6 1.3 collective-permute-start.1
  421.9 27.7 %all_gather.11 = bf16[2,5120,32]{1,2,0:T(8,128)(2,1)S(1)} all-gather(bf16[2,640,32]{1,2,0:T(8,128)(2,1)S(1)} %fusion.29), channel_id=1, replica_groups=mesh['role'=2,'dp'=2,'hidden'=8] {'hidden'}, dimensions={1}, use_global_device_ids=true | all-gather | bytes 737280 | tf_op jit(solution)/shard_map/all_gather | solution.py:126
  449.6 0.8 copy-done.6
  450.4 0.1 fusion.19
  450.4 14.6 %fusion.7 = f32[128,1728]{0,1:T(8,128)} fusion(bf16[2,5120,1728]{1,2,0:T(8,128)(2,1)} %all-gather.3.cloned.1.call-done, bf16[1,128,5120]{2,1,0:T(8,128)(2,1)S(1)} %copy-done, bf16[2,5120,32]{1,2,0:T(8,128)(2,1)S(1)} %all_gather.11, bf16[2,32,1728]{2,1,0:T(8,128)(2,1)S(1)} %fusion.19), kind=kOutput, calls=%fused_computation.16 | convolution fusion | flops 2866544640 | bytes 20332544 | tf_op jit(solution)/shard_map/dot_general | solution.py:139
  465.0 14.6 %fusion.8 = bf16[128,1728]{0,1:T(8,128)(2,1)} fusion(bf16[2,5120,1728]{1,2,0:T(8,128)(2,1)} %all-gather.3.cloned.1.call-done, bf16[1,128,5120]{2,1,0:T(8,128)(2,1)S(1)} %copy-done, f32[128,1728]{0,1:T(8,128)} %fusion.7, bf16[2,5120,32]{1,2,0:T(8,128)(2,1)S(1)} %all_gather.11, bf16[2,32,1728]{2,1,0:T(8,128)(2,1)S(1)} %fusion.19), kind=kOutput, calls=%fused_computation.17 | convolution fusion | flops 2867871744 | bytes 20774912 | tf_op jit(solution)/shard_map/dot_general | solution.py:139
  479.6 8.8 %convolution_convert_fusion = bf16[128,5120]{1,0:T(8,128)(2,1)S(1)} fusion(bf16[128,1728]{0,1:T(8,128)(2,1)} %fusion.8, bf16[1728,5120]{1,0:T(8,128)(2,1)} %all-gather.5.cloned.1.call-done), kind=kOutput, calls=%fused_computation.8 | convolution fusion | flops 2265579520 | bytes 19447808 | tf_op jit(solution)/shard_map/dot_general | solution.py:38
  488.5 1.5 copy.22
  490.7 3.6 collective-permute-start.2
  494.3 1.3 collective-permute-start.3
  495.7 1.3 collective-permute-start.4
  497.0 1.3 collective-permute-start.5
  498.3 1.6 fusion.28
  499.9 1.6 select_bitcast_fusion.3
  501.5 1.6 select_bitcast_fusion.2
  503.1 0.8 fusion.18
  504.0 1.0 collective-permute-done.4
  505.0 0.8 select_bitcast_fusion.1
  505.8 8.9 %collective-permute-done.5 = f32[2,32,1728]{2,1,0:T(8,128)S(1)} collective-permute-done((f32[2,32,1728]{2,1,0:T(8,128)S(1)}, f32[2,32,1728]{2,1,0:T(8,128)S(1)}, u32[]{:S(2)}, u32[]{:S(2)}) %collective-permute-start.5) | collective-permute-done | bytes 442400 | tf_op jit(solution)/shard_map/ppermute | solution.py:21
  514.7 0.8 select_bitcast_fusion
  515.5 1.1 copy.21
  516.6 43.9 %reduce-scatter.9.cloned.1.call-done = bf16[640,128]{1,0:T(8,128)(2,1)} async-done(((bf16[5120,128]{1,0:T(8,128)(2,1)}), bf16[640,128]{1,0:T(8,128)(2,1)}) %reduce-scatter.9.cloned.1.call-update) | async-done | bytes 163856
  560.5 1.1 copy.23
  561.6 0.8 select_bitcast_fusion.4
  (46 shorter events, 0.4 us)
Async XLA Ops:
  7.2 1.7 copy-start
  7.2 118.4 %all-gather.5.cloned.1.call-start = ((), (), s32[]{:S(2)}) async-start(), calls=%async_computation.3 | async-start | bytes 22118400 | tf_op jit(solution)/shard_map/all_gather | solution.py:68
  7.9 0.9 copy-start.10
  7.9 32.2 %copy-start.15 = (s32[128]{0:T(128)S(1)}, s32[128]{0:T(128)}, u32[]{:S(2)}) copy-start(s32[128]{0:T(128)} %param.16) | copy-start | bytes 1540
  7.9 333.4 %all-gather.3.cloned.1.call-start = ((), (), s32[]{:S(2)}) async-start(), calls=%async_computation.2 | async-start | bytes 44236800 | tf_op jit(solution)/shard_map/all_gather | solution.py:66
  8.7 404.4 %all-reduce.3.cloned.1.call-start = ((), (), s32[]{:S(2)}) async-start(), calls=%async_computation.6 | async-start | bytes 1245184 | tf_op jit(solution)/shard_map/psum | solution.py:113
  134.1 207.2 %copy-start.1 = (f32[128,1728]{0,1:T(8,128)}, f32[128,1728]{0,1:T(8,128)S(1)}, u32[]{:S(2)}) copy-start(f32[128,1728]{0,1:T(8,128)S(1)} %get-tuple-element.31) | copy-start | bytes 2654212
  341.3 15.3 %copy-start.4 = (f32[2,32,1728]{2,1,0:T(8,128)S(1)}, f32[2,32,1728]{2,1,0:T(8,128)}, u32[]{:S(2)}) copy-start(f32[2,32,1728]{2,1,0:T(8,128)} %param.21) | copy-start | bytes 1327108
  356.6 1.2 copy-start.2
  390.5 125.0 %reduce-scatter.7.cloned.1.call-start = ((), (), s32[]{:S(2)}) async-start(), calls=%async_computation.4 | async-start | bytes 1474560
  400.3 12.8 %copy-start.11 = (f32[2,640,32]{1,2,0:T(8,128)S(1)}, f32[2,640,32]{1,2,0:T(8,128)}, u32[]{:S(2)}) copy-start(f32[2,640,32]{1,2,0:T(8,128)} %param.20) | copy-start | bytes 491524
  400.3 12.8 %copy-start.13 = (f32[2,640,32]{1,2,0:T(8,128)S(1)}, f32[2,640,32]{1,2,0:T(8,128)}, u32[]{:S(2)}) copy-start(f32[2,640,32]{1,2,0:T(8,128)} %param.22) | copy-start | bytes 491524
  400.3 12.8 %copy-start.14 = (f32[2,640,32]{1,2,0:T(8,128)S(1)}, f32[2,640,32]{1,2,0:T(8,128)}, u32[]{:S(2)}) copy-start(f32[2,640,32]{1,2,0:T(8,128)} %param.23) | copy-start | bytes 491524
  400.3 18.0 %copy-start.5 = (f32[2,32,1728]{2,1,0:T(8,128)S(1)}, f32[2,32,1728]{2,1,0:T(8,128)}, u32[]{:S(2)}) copy-start(f32[2,32,1728]{2,1,0:T(8,128)} %param.21) | copy-start | bytes 1327108
  400.3 18.0 %copy-start.12 = (f32[2,32,1728]{2,1,0:T(8,128)S(1)}, f32[2,32,1728]{2,1,0:T(8,128)}, u32[]{:S(2)}) copy-start(f32[2,32,1728]{2,1,0:T(8,128)} %param.24) | copy-start | bytes 1327108
  402.9 157.6 %reduce-scatter.9.cloned.1.call-start = ((), (), s32[]{:S(2)}) async-start(), calls=%async_computation.5 | async-start | bytes 1474560
  414.9 34.7 %copy-start.8 = (f32[2,640,32]{1,2,0:T(8,128)}, f32[2,640,32]{1,2,0:T(8,128)S(1)}, u32[]{:S(2)}) copy-start(f32[2,640,32]{1,2,0:T(8,128)S(1)} %get-tuple-element.22) | copy-start | bytes 491524
  414.9 7.0 %collective-permute-start = (f32[2,640,32]{1,2,0:T(8,128)S(1)}, f32[2,640,32]{1,2,0:T(8,128)S(1)}, u32[]{:S(2)}, u32[]{:S(2)}) collective-permute-start(f32[2,640,32]{1,2,0:T(8,128)S(1)} %get-tuple-element.22), channel_id=1, source_target_pairs={{0,16},{1,17},{2,18},{3,19},{4,20},{5,21},{6,22},{7,23},{8,24},{9,... | collective-permute-start | bytes 491528 | tf_op jit(solution)/shard_map/ppermute | solution.py:21
  420.6 29.0 %collective-permute-start.1 = (f32[2,32,1728]{2,1,0:T(8,128)S(1)}, f32[2,32,1728]{2,1,0:T(8,128)S(1)}, u32[]{:S(2)}, u32[]{:S(2)}) collective-permute-start(f32[2,32,1728]{2,1,0:T(8,128)S(1)} %get-tuple-element.19), channel_id=1, source_target_pairs={{0,16},{1,17},{2,18},{3,19},{4,20},{5,21},{6,22},{7,23},{8,24},{9,... | collective-permute-start | bytes 1327112 | tf_op jit(solution)/shard_map/ppermute | solution.py:21
  421.9 27.7 %copy-start.9 = (f32[2,640,32]{1,2,0:T(8,128)}, f32[2,640,32]{1,2,0:T(8,128)S(1)}, u32[]{:S(2)}) copy-start(f32[2,640,32]{1,2,0:T(8,128)S(1)} %collective-permute-done) | copy-start | bytes 491524
  449.6 0.8 copy-start.6
  490.0 13.2 %copy-start.7 = (f32[2,32,1728]{2,1,0:T(8,128)S(1)}, f32[2,32,1728]{2,1,0:T(8,128)}, u32[]{:S(2)}) copy-start(f32[2,32,1728]{2,1,0:T(8,128)} %copy-done.6) | copy-start | bytes 1327108
  490.0 15.0 %copy-start.3 = (f32[2,32,1728]{2,1,0:T(8,128)S(1)}, f32[2,32,1728]{2,1,0:T(8,128)}, u32[]{:S(2)}) copy-start(f32[2,32,1728]{2,1,0:T(8,128)} %get-tuple-element.20) | copy-start | bytes 1327108
  490.7 9.2 %collective-permute-start.2 = (f32[2,640,32]{1,2,0:T(8,128)}, f32[2,640,32]{1,2,0:T(8,128)S(1)}, u32[]{:S(2)}, u32[]{:S(2)}) collective-permute-start(f32[2,640,32]{1,2,0:T(8,128)} %get-tuple-element.23), channel_id=1, source_target_pairs={{0,16},{1,17},{2,18},{3,19},{4,20},{5,21},{6,22},{7,23},{8,24},{9,... | collective-permute-start | bytes 491528 | tf_op jit(solution)/shard_map/ppermute | solution.py:21
  494.3 7.2 %collective-permute-start.3 = (f32[2,640,32]{1,2,0:T(8,128)}, f32[2,640,32]{1,2,0:T(8,128)S(1)}, u32[]{:S(2)}, u32[]{:S(2)}) collective-permute-start(f32[2,640,32]{1,2,0:T(8,128)} %get-tuple-element.24), channel_id=1, source_target_pairs={{0,16},{1,17},{2,18},{3,19},{4,20},{5,21},{6,22},{7,23},{8,24},{9,... | collective-permute-start | bytes 491528 | tf_op jit(solution)/shard_map/ppermute | solution.py:21
  495.7 9.3 %collective-permute-start.4 = (f32[2,32,1728]{2,1,0:T(8,128)}, f32[2,32,1728]{2,1,0:T(8,128)S(1)}, u32[]{:S(2)}, u32[]{:S(2)}) collective-permute-start(f32[2,32,1728]{2,1,0:T(8,128)} %get-tuple-element.20), channel_id=1, source_target_pairs={{0,16},{1,17},{2,18},{3,19},{4,20},{5,21},{6,22},{7,23},{8,24},{9,... | collective-permute-start | bytes 1327112 | tf_op jit(solution)/shard_map/ppermute | solution.py:21
  497.0 17.7 %collective-permute-start.5 = (f32[2,32,1728]{2,1,0:T(8,128)S(1)}, f32[2,32,1728]{2,1,0:T(8,128)S(1)}, u32[]{:S(2)}, u32[]{:S(2)}) collective-permute-start(f32[2,32,1728]{2,1,0:T(8,128)S(1)} %get-tuple-element.21), channel_id=1, source_target_pairs={{0,16},{1,17},{2,18},{3,19},{4,20},{5,21},{6,22},{7,23},{8,24},{9,... | collective-permute-start | bytes 1327112 | tf_op jit(solution)/shard_map/ppermute | solution.py:21
Sparse Core Ops, SparseCore 0:
  9.6 115.9 all-gather.4
  127.2 214.1 all-gather.2
  390.6 22.4 all-reduce.2
  416.4 65.1 reduce-scatter.6
  490.1 70.3 reduce-scatter.8
where the time goes:
time: 571 us; the launch traced here: 569 us
  waiting for transfers between devices  356 us (62%)
  blocking collectives  88.6 us (16%)
  matrix products  74.5 us (13%)
  between operations  14.8 us (3%)
  other arithmetic  14.4 us (3%)
  starting transfers between devices  12.5 us (2%)
  local copies, waits for them, and re-layouts  7.81 us (1%)
    all_gather x1, waiting for transfers between devices, local(): lax.all_gather(frozen_gate_up_weight, ('role', 'dp'), axis=1, tiled=True)  207 us
    all_gather x1, waiting for transfers between devices, local(): full_down = lax.all_gather(down_weight, ('role', 'dp'), axis=1, tiled=True)  83.7 us
    unnamed x7, waiting for transfers between devices  45.3 us
    psum x1, blocking collectives, local(): reduced_gradient = lax.psum(reduced_part, 'hidden').astype(jnp.bfloat16)  31.1 us
    psum x1, blocking collectives, local(): passed_through = lax.psum(through_part, 'hidden').astype(jnp.bfloat16)  29.9 us
    dot_general x2, matrix products, local(): jnp.dot(token_batch, merged_weight, preferred_element_type=jnp.float32)  29.2 us
    all_gather x1, blocking collectives, local(): lax.all_gather(new_in.astype(jnp.bfloat16), 'hidden', axis=1, tiled=True)  27.7 us
    dot_general x2, matrix products, finish(): jnp.dot(hidden_act, full_down, preferred_element_type=jnp.float32)  18.6 us
  transfers between devices with their start and end apart: 11, of which 6 were waited for; matrix products, arithmetic and copies ran while one was open for 13% of the time, Pallas kernels for 0%

commit v1 on v0

v1 whole, which is shorter than its diff:
```python
import functools

import jax
import jax.numpy as jnp
from jax import lax
from jax.experimental import pallas as pl
from jax.experimental.pallas import tpu as pltpu
from jax.sharding import PartitionSpec as P

OPT_STEP = 10
ADAPTER_SCALE = 2.0
BETA_ONE = 0.9
BETA_TWO = 0.999
RATE_FACTOR = 0.34
ADAM_EPS = 1e-08
KEEP_RATE = 0.75

MESH = pl.DeviceIdType.MESH
VMEM_LIMIT = 48 * 1024 * 1024
F32 = jnp.float32
BF16 = jnp.bfloat16


def adam_update(param, grad, first, second, width):
    learn_rate = RATE_FACTOR / width**0.5
    first_new = BETA_ONE * first + (1.0 - BETA_ONE) * grad
    second_new = BETA_TWO * second + (1.0 - BETA_TWO) * grad * grad
    first_fix = first_new / (1.0 - BETA_ONE**OPT_STEP)
    second_fix = second_new / (1.0 - BETA_TWO**OPT_STEP)
    return (
        param - learn_rate * first_fix / (jnp.sqrt(second_fix) + ADAM_EPS),
        first_new,
        second_new,
    )


def shape_of(shape, dtype):
    return jax.ShapeDtypeStruct(shape, dtype)


def ring(index, step, size):
    return lax.rem(index + step, size)


def remote(src, dst, sems, slot, device):
    send, recv = sems
    return pltpu.make_async_remote_copy(
        src_ref=src,
        dst_ref=dst,
        send_sem=send.at[slot],
        recv_sem=recv.at[slot],
        device_id=device,
        device_id_type=MESH,
    )


def greet(peers):
    barrier = pltpu.get_barrier_semaphore()
    for peer in peers:
        pl.semaphore_signal(barrier, inc=1, device_id=peer, device_id_type=MESH)
    pl.semaphore_wait(barrier, len(peers))


def hidden_peers(hidden):
    me = lax.axis_index("hidden")
    return [{"hidden": ring(me, step, hidden)} for step in range(1, hidden)]


def dp_peers(n_dp):
    me = lax.axis_index("dp")
    return [{"dp": ring(me, step, n_dp)} for step in range(1, n_dp)]


def other_role():
    return {"role": 1 - lax.axis_index("role")}


def call(body, outs, scratch, cid, *operands):
    spec = pl.BlockSpec(memory_space=pltpu.VMEM)
    return pl.pallas_call(
        body,
        out_shape=outs,
        in_specs=[spec] * len(operands),
        out_specs=[spec] * len(outs),
        scratch_shapes=scratch,
        compiler_params=pltpu.CompilerParams(
            collective_id=cid, has_side_effects=True, vmem_limit_bytes=VMEM_LIMIT
        ),
    )(*operands)


def dma_pair(count):
    return [pltpu.SemaphoreType.DMA((count,)), pltpu.SemaphoreType.DMA((count,))]


def spread_kernel(sizes, tok, up, red, tok_all, up_all, red_all, s0, r0, s1, r1, s2, r2):
    n_role, n_dp, hidden = sizes
    role, dp, me = (lax.axis_index(a) for a in ("role", "dp", "hidden"))
    group = [
        (ring(role, a, n_role), ring(dp, b, n_dp))
        for a in range(n_role)
        for b in range(n_dp)
        if a or b
    ]
    greet([{"role": a, "dp": b} for a, b in group] + hidden_peers(hidden))
    copies = []
    own = dp * n_role + role
    for slot, (a, b) in enumerate(group):
        copies.append(
            remote(tok.at[a * n_dp + b], tok_all.at[own], (s0, r0), slot, {"role": a, "dp": b})
        )
    for slot, peer in enumerate(dp_peers(n_dp)):
        copies.append(remote(up.at[role * n_dp + peer["dp"]], up_all.at[dp], (s1, r1), slot, peer))
    for slot, peer in enumerate(hidden_peers(hidden)):
        copies.append(remote(red, red_all.at[me], (s2, r2), slot, peer))
    for copy in copies:
        copy.start()
    tok_all[own] = tok[role * n_dp + dp]
    up_all[dp] = up[role * n_dp + dp]
    red_all[me] = red[...]
    for copy in copies:
        copy.wait()


def reduce_kernel(sizes, part, grad, base, grad_sum, got, got_grad, out_part, out_grad, far, far_grad,
                  s0, r0, s1, r1, s2, r2, s3, r3):
    n_role, n_dp, _ = sizes
    role, dp = lax.axis_index("role"), lax.axis_index("dp")
    greet(dp_peers(n_dp) + [other_role()])
    copies = []
    for slot, peer in enumerate(dp_peers(n_dp)):
        copies.append(remote(part.at[:, peer["dp"]], got.at[slot], (s0, r0), slot, peer))
        copies.append(remote(grad.at[peer["dp"]], got_grad.at[slot], (s1, r1), slot, peer))
    for copy in copies:
        copy.start()
    for copy in copies:
        copy.wait()
    rows = base.shape[1]
    step = 16

    @pl.loop(0, rows // step)
    def _(i):
        at = pl.ds(pl.multiple_of(i * step, step), step)
        for k in range(2):
            total = part[k, dp, 1 - role, at].astype(F32)
            for slot in range(n_dp - 1):
                total = total + got[slot, k, 1 - role, at].astype(F32)
            out_part[k, at] = total.astype(BF16)
        total = grad[dp, at].astype(F32)
        for slot in range(n_dp - 1):
            total = total + got_grad[slot, at].astype(F32)
        out_grad[at] = total.astype(BF16)

    across = remote(out_part, far, (s2, r2), 0, other_role())
    across_grad = remote(out_grad, far_grad, (s3, r3), 0, other_role())
    across.start()

    @pl.when(role == 1)
    def _():
        across_grad.start()
        across_grad.wait_send()

    @pl.when(role == 0)
    def _():
        across_grad.wait_recv()

    across.wait()
    keep = jnp.where(role == 0, 1.0, 0.0).astype(F32)

    @pl.loop(0, rows // step)
    def _(i):
        at = pl.ds(pl.multiple_of(i * step, step), step)
        for k in range(2):
            total = part[k, dp, role, at].astype(F32)
            for slot in range(n_dp - 1):
                total = total + got[slot, k, role, at].astype(F32)
            base[k, at] = total + far[k, at].astype(F32)

        @pl.when(role == 0)
        def _():
            grad_sum[at] = out_grad[at].astype(F32) + far_grad[at].astype(F32)

        @pl.when(role == 1)
        def _():
            grad_sum[at] = jnp.zeros_like(grad_sum[at])


def share_kernel(sizes, with_hidden, with_gather, with_grad, *refs):
    n_role, n_dp, hidden = sizes
    role, dp, me = (lax.axis_index(a) for a in ("role", "dp", "hidden"))
    refs = list(refs)
    n_jobs = with_hidden + with_gather + with_grad
    ins, outs, sems = refs[:n_jobs], refs[n_jobs : 2 * n_jobs], refs[2 * n_jobs :]
    peers = []
    if with_hidden:
        peers += hidden_peers(hidden)
    if with_gather or with_grad:
        peers += dp_peers(n_dp) + [other_role()]
    greet(peers)
    waits = []
    if with_hidden:
        src, dst, pair = ins.pop(0), outs.pop(0), (sems.pop(0), sems.pop(0))
        for slot, peer in enumerate(hidden_peers(hidden)):
            copy = remote(src, dst.at[me], pair, slot, peer)
            copy.start()
            waits.append(copy)
        dst[me] = src[...]
    if with_grad:
        grad_src, grad_dst = ins.pop(), outs.pop()
        g_near, g_far = (sems.pop(-2), sems.pop()), (sems.pop(-2), sems.pop())
        grad_over = remote(grad_src, grad_dst.at[dp], g_far, 0, other_role())

        @pl.when(role == 0)
        def _():
            grad_over.start()
            grad_dst[dp] = grad_src[...]

    if with_gather:
        src, dst = ins.pop(0), outs.pop(0)
        near, far = (sems.pop(0), sems.pop(0)), (sems.pop(0), sems.pop(0))
        over = remote(src, dst.at[dp, role], far, 0, other_role())
        over.start()
        dst[dp, role] = src[...]
    if with_grad:

        @pl.when(role == 0)
        def _():
            grad_over.wait_send()

        @pl.when(role == 1)
        def _():
            grad_over.wait_recv()

        for slot, peer in enumerate(dp_peers(n_dp)):
            copy = remote(grad_dst.at[dp], grad_dst.at[dp], g_near, slot, peer)
            copy.start()
            waits.append(copy)
    if with_gather:
        over.wait()
        for slot, peer in enumerate(dp_peers(n_dp)):
            copy = remote(dst.at[dp], dst.at[dp], near, slot, peer)
            copy.start()
            waits.append(copy)
    for copy in waits:
        copy.wait()


def share(sizes, cid, hidden_in=None, gather_in=None, grad_in=None):
    n_role, n_dp, hidden = sizes
    operands, outs, scratch = [], [], []
    if hidden_in is not None:
        operands.append(hidden_in)
        outs.append(shape_of((hidden,) + hidden_in.shape, hidden_in.dtype))
        scratch += dma_pair(hidden - 1)
    if gather_in is not None:
        operands.append(gather_in)
        outs.append(shape_of((n_dp, n_role) + gather_in.shape, gather_in.dtype))
        scratch += dma_pair(n_dp - 1) + dma_pair(1)
    if grad_in is not None:
        operands.append(grad_in)
        outs.append(shape_of((n_dp,) + grad_in.shape, grad_in.dtype))
        scratch += dma_pair(1) + dma_pair(n_dp - 1)
    body = functools.partial(
        share_kernel, sizes, hidden_in is not None, gather_in is not None, grad_in is not None
    )
    return call(body, outs, scratch, cid, *operands)


def finish_kernel(sizes, part, out, got, summed, far, result, s0, r0, s1, r1, s2, r2):
    n_role, n_dp, hidden = sizes
    role, dp, me = (lax.axis_index(a) for a in ("role", "dp", "hidden"))
    pairs = hidden // 2
    pair, odd = me // 2, lax.rem(me, 2)
    mine = role * n_dp + dp
    t_role, t_dp = pair // n_dp, lax.rem(pair, n_dp)
    owner = {"role": t_role, "dp": t_dp, "hidden": mine * 2 + odd}
    others = [{"hidden": ring(pair, step, pairs) * 2 + odd} for step in range(1, pairs)]
    mate = {"hidden": pair * 2 + 1 - odd}
    barrier = pltpu.get_barrier_semaphore()
    for peer in others + [mate]:
        pl.semaphore_signal(barrier, inc=1, device_id=peer, device_id_type=MESH)

    @pl.when(mine != pair)
    def _():
        pl.semaphore_signal(barrier, inc=1, device_id=owner, device_id_type=MESH)

    pl.semaphore_wait(barrier, jnp.where(mine != pair, pairs + 1, pairs))

    order = list(range(1, pairs)) + [0]
    firsts = []
    for step in order:
        block = ring(pair, step, pairs)
        copy = remote(part.at[block, 1 - odd], got.at[block], (s0, r0), step, mate)
        firsts.append((step, block, copy))
    for _, _, copy in firsts:
        copy.start()
    seconds = []
    for step, block, copy in firsts:
        copy.wait()
        total = part[block, odd].astype(F32) + got[block].astype(F32)
        summed[block] = total.astype(BF16)
        if step:
            copy = remote(summed.at[block], far.at[step - 1], (s1, r1), step - 1, others[step - 1])
            copy.start()
            seconds.append(copy)
    total = summed[pair].astype(F32)
    for step, copy in enumerate(seconds):
        copy.wait()
        total = total + far[step].astype(F32)
    result[...] = total.astype(BF16)
    last = remote(result, out, (s2, r2), 0, owner)

    @pl.when(mine != pair)
    def _():
        last.start()
        last.wait()

    @pl.when(mine == pair)
    def _():
        out[...] = result[...]


def finish(sizes, cid, hidden_all, down_weight, live):
    n_role, n_dp, hidden = sizes
    rows = hidden_all.shape[2]
    width = down_weight.shape[1]
    per = hidden // (n_role * n_dp)
    part = jnp.einsum("grf,fd->grd", hidden_all.reshape((-1,) + hidden_all.shape[2:]), down_weight,
                      preferred_element_type=F32).astype(BF16)
    part = part.reshape(n_dp, n_role, rows, per, width // per)
    part = part.transpose(1, 0, 3, 2, 4).reshape(n_role * n_dp, per, rows, width // per)
    pairs = hidden // 2
    block = (rows, width // per)
    (out,) = call(
        functools.partial(finish_kernel, sizes),
        [shape_of(block, BF16)],
        [
            pltpu.VMEM((pairs,) + block, BF16),
            pltpu.VMEM((pairs,) + block, BF16),
            pltpu.VMEM((pairs - 1,) + block, BF16),
            pltpu.VMEM(block, BF16),
        ]
        + dma_pair(pairs)
        + dma_pair(pairs - 1)
        + dma_pair(1),
        cid,
        part,
    )
    return jnp.where(live[:, None], out, jnp.zeros_like(out))


def local(
    sizes,
    token_rows,
    cotangent,
    staleness,
    prefill_rows,
    frozen_gate_up_weight,
    down_weight,
    adapter_in,
    adapter_out,
    moment_in,
    square_in,
    moment_out,
    square_out,
):
    n_role, n_dp, hidden = sizes
    groups = n_role * n_dp
    half_index = lax.axis_index("role")
    shard_index = lax.axis_index("hidden")
    token_batch = token_rows[0]
    rows, model = token_batch.shape
    part_width = adapter_in.shape[1]
    rank = adapter_in.shape[2]
    units = frozen_gate_up_weight.shape[2]
    width = frozen_gate_up_weight.shape[1]
    positions = jnp.arange(rows)
    live = jnp.logical_or(half_index == 0, positions < prefill_rows[0])

    token_part = lax.dynamic_slice_in_dim(token_batch, shard_index * part_width, part_width, 1)
    reduced_part = jnp.einsum(
        "rd,kdq->krq", token_part, adapter_in.astype(BF16), preferred_element_type=F32
    )
    row_weight = KEEP_RATE ** staleness.astype(F32)
    upstream = (row_weight[:, None] * cotangent.astype(F32)).astype(BF16)

    def blocked(value):
        return value.reshape(rows, groups, width).transpose(1, 0, 2)

    tokens_all, upstream_all, reduced_all = call(
        functools.partial(spread_kernel, sizes),
        [
            shape_of((groups, rows, width), BF16),
            shape_of((n_dp, rows, width), BF16),
            shape_of((hidden, 2, rows, rank), F32),
        ],
        dma_pair(groups - 1) + dma_pair(n_dp - 1) + dma_pair(hidden - 1),
        1,
        blocked(token_batch),
        blocked(upstream),
        reduced_part,
    )
    products = jnp.einsum(
        "rd,kdf->krf",
        tokens_all.reshape(groups * rows, width),
        frozen_gate_up_weight,
        preferred_element_type=F32,
    ).astype(BF16).reshape(2, n_dp, n_role, rows, units)
    grad_products = lax.dot_general(
        upstream_all.reshape(n_dp * rows, width),
        down_weight,
        (((1,), (1,)), ((), ())),
        preferred_element_type=F32,
    ).astype(BF16).reshape(n_dp, rows, units)
    base, grad_hidden = call(
        functools.partial(reduce_kernel, sizes),
        [shape_of((2, rows, units), F32), shape_of((rows, units), F32)],
        [
            pltpu.VMEM((n_dp - 1, 2, n_role, rows, units), BF16),
            pltpu.VMEM((n_dp - 1, rows, units), BF16),
            pltpu.VMEM((2, rows, units), BF16),
            pltpu.VMEM((rows, units), BF16),
            pltpu.VMEM((2, rows, units), BF16),
            pltpu.VMEM((rows, units), BF16),
        ]
        + dma_pair(n_dp - 1)
        + dma_pair(n_dp - 1)
        + dma_pair(1)
        + dma_pair(1),
        2,
        products,
        grad_products,
    )
    reduced = reduced_all.sum(axis=0).astype(BF16)
    out_bf = adapter_out.astype(BF16)
    pre = base + ADAPTER_SCALE * jnp.einsum(
        "krq,kqf->krf", reduced, out_bf, preferred_element_type=F32
    )
    sigma = jax.nn.sigmoid(pre[0])
    hidden_old = (pre[0] * sigma * pre[1]).astype(BF16)
    grad_gate = (grad_hidden * pre[1] * sigma * (1.0 + pre[0] * (1.0 - sigma))).astype(BF16)
    grad_up = (grad_hidden * pre[0] * sigma).astype(BF16)
    grads = jnp.stack([grad_gate, grad_up])
    partial_out = ADAPTER_SCALE * jnp.einsum(
        "krq,krf->kqf", reduced, grads, preferred_element_type=F32
    )
    through_part = jnp.einsum("krf,kqf->krq", grads, out_bf, preferred_element_type=F32)
    through_all, hidden_old_all, grad_out_all = share(
        sizes, 3, through_part, hidden_old, partial_out
    )
    through = through_all.sum(axis=0).astype(BF16)
    partial_in = ADAPTER_SCALE * jnp.einsum(
        "un,huj->hnj", token_part, through, preferred_element_type=F32
    )
    (grad_in_all,) = share(sizes, 4, None, None, partial_in)
    grad_in = grad_in_all.sum(axis=0)
    grad_out = grad_out_all.sum(axis=0)
    new_in, new_m_in, new_s_in = adam_update(adapter_in, grad_in, moment_in, square_in, model)
    new_out, new_m_out, new_s_out = adam_update(
        adapter_out, grad_out, moment_out, square_out, model
    )
    new_part = jnp.einsum(
        "rd,kdq->krq", token_part, new_in.astype(BF16), preferred_element_type=F32
    )
    (new_all,) = share(sizes, 5, new_part)
    new_reduced = new_all.sum(axis=0).astype(BF16)
    post = base + ADAPTER_SCALE * jnp.einsum(
        "krq,kqf->krf", new_reduced, new_out.astype(BF16), preferred_element_type=F32
    )
    hidden_new = (jax.nn.silu(post[0]) * post[1]).astype(BF16)
    (hidden_new_all,) = share(sizes, 6, None, hidden_new)
    layer_old = finish(sizes, 7, hidden_old_all, down_weight, live)
    layer_new = finish(sizes, 8, hidden_new_all, down_weight, live)
    return (
        layer_old[None],
        layer_new[None],
        new_in[None],
        new_out[None],
        new_m_in[None],
        new_s_in[None],
        new_m_out[None],
        new_s_out[None],
    )


def solution(mesh):
    in_specs = (
        P("role", "dp", None),
        P("dp", None),
        P("dp"),
        P("dp"),
        P(None, ("role", "dp"), "hidden"),
        P("hidden", ("role", "dp")),
        P(None, "hidden", None),
        P(None, None, "hidden"),
        P(None, "hidden", None),
        P(None, "hidden", None),
        P(None, None, "hidden"),
        P(None, None, "hidden"),
    )
    out_specs = (
        P("role", "dp", "hidden"),
        P("role", "dp", "hidden"),
        P("role", None, "hidden", None),
        P("role", None, None, "hidden"),
        P("role", None, "hidden", None),
        P("role", None, "hidden", None),
        P("role", None, None, "hidden"),
        P("role", None, None, "hidden"),
    )
    sizes = tuple(mesh.shape[axis] for axis in ("role", "dp", "hidden"))
    return jax.shard_map(
        functools.partial(local, sizes),
        mesh=mesh,
        in_specs=in_specs,
        out_specs=out_specs,
        check_vma=False,
    )
```

time: 571 us -> 282 us (0.49)
  waiting for transfers between devices: 356 us -> 0 us
  Pallas kernels: 0 us -> 217 us
  blocking collectives: 88.6 us -> 0 us
  matrix products: 74.5 us -> 25.6 us
  local copies, waits for them, and re-layouts: 7.81 us -> 24.5 us
  between operations: 14.8 us -> 1.61 us
  starting transfers between devices: 12.5 us -> 0 us
    all_gather x2 -> x0, waiting for transfers between devices: 291 us -> none  [the longest x1 207 us: local(): lax.all_gather(frozen_gate_up_weight, ('role', 'dp'), axis=1, tiled=True)]
    pallas_call x0 -> x8, Pallas kernels: none -> 217 us  [call(): pl.pallas_call(body, out_shape=outs, in_specs=[spec] * len(operands), out...]
    psum x2 -> x0, blocking collectives: 61 us -> none  [the longest x1 31.1 us: local(): reduced_gradient = lax.psum(reduced_part, 'hidden').astype(jnp.bfloat16)]
    dot_general x10, matrix products: 74.3 us -> 24.5 us  [the longest x1 9.79 us: local(): jnp.einsum('rd,kdf->krf', tokens_all.reshape(groups * rows, width), froze...]
    unnamed x7 -> x0, waiting for transfers between devices: 45.3 us -> none
    all_gather x1 -> x0, blocking collectives: 27.7 us -> none  [local(): lax.all_gather(new_in.astype(jnp.bfloat16), 'hidden', axis=1, tiled=True)]
    ppermute x6 -> x0, starting transfers between devices: 12.3 us -> none  [from_behind(): lax.ppermute(value, axis, [(source, source + steps) for source in range(f...]
    psum x1 -> x0, waiting for transfers between devices: 10.1 us -> none  [local(): lax.psum((partial_in_gradient, partial_out_gradient), 'dp')]
  transfers between devices with their start and end apart: 11 -> 0, of which waited for: 6 -> 0; matrix products, arithmetic and copies ran while one was open for 13% -> 0% of each run, Pallas kernels for 0% -> 0%
where the time goes in v1:
time: 282 us; the launch traced here: 281 us
  Pallas kernels  217 us (77%)
  matrix products  25.6 us (9%)
  local copies, waits for them, and re-layouts  24.5 us (9%)
  other arithmetic  12.8 us (5%)
    pallas_call x8, Pallas kernels, call(): pl.pallas_call(body, out_shape=outs, in_specs=[spec] * len(operands), out...  217 us
    dot_general x1, matrix products, local(): jnp.einsum('rd,kdf->krf', tokens_all.reshape(groups * rows, width), froze...  9.79 us
    unnamed x24, local copies, waits for them, and re-layouts  7.52 us
    dot_general x2, matrix products, finish(): jnp.einsum('grf,fd->grd', hidden_all.reshape((-1,) + hidden_all.shape[2:]...  6.14 us
    reshape x4, local copies, waits for them, and re-layouts, finish(): part = part.reshape(n_dp, n_role, rows, per, width // per)  5.84 us
    convert_element_type x1, local copies, waits for them, and re-layouts, local(): products = jnp.einsum('rd,kdf->krf', tokens_all.reshape(groups * rows, wi...  5.83 us

profile of v1, /device:TPU:1, one launch (start us, length us, event | category | flops | bytes accessed | tf_op | source)
XLA Modules:
  0.0 281.1 jit_solution(18091147032341011663)
XLA Ops:
  1.3 0.7 convert_power_fusion
  2.0 0.9 convert_element_type.60
  2.9 1.1 fusion.24
  4.0 0.1 copy.83
  4.1 1.8 copy.81
  5.9 0.3 multiply_convert_fusion
  6.2 0.6 copy.82
  6.8 2.4 copy.79
  9.2 1.6 copy.80
  10.8 21.9 %shard_map.179 = (bf16[4,128,1280]{2,1,0:T(8,128)(2,1)S(1)}, bf16[2,128,1280]{2,1,0:T(8,128)(2,1)S(1)}, f32[8,2,128,32]{3,2,1,0:T(8,128)S(1)}) custom-call(bf16[4,128,1280]{2,1,0:T(8,128)(2,1)S(1)} %bitcast.108, bf16[4,128,1280]{2,1,0:T(8,128)(2,1)S(1)} %bitcast.107, f32[2,128,32]{2,1,0:T(8,128)S(1)} %bitcast.113), custom_call_target="tpu_custom_call" | custom-call | tf_op jit(solution)/shard_map/pallas_call | solution.py:80
  32.7 1.0 copy-done
  33.7 1.1 copy-done.2
  34.8 1.3 reduce_sum.45
  36.2 4.6 %convolution_convert_fusion.1 = bf16[256,1728]{0,1:T(8,128)(2,1)} fusion(bf16[256,1280]{1,0:T(8,128)(2,1)S(1)} %bitcast.116, bf16[1728,1280]{1,0:T(8,128)(2,1)} %param.17), kind=kOutput, calls=%fused_computation.13 | convolution fusion | flops 1132904448 | bytes 5963776 | tf_op jit(solution)/shard_map/dot_general | solution.py:409
  40.8 1.4 copy.85
  42.2 9.8 %fusion.4 = bf16[2,512,1728]{1,2,0:T(8,128)(2,1)} fusion(bf16[512,1280,1]{1,0,2:T(8,128)(2,1)S(1)} %bitcast.115, bf16[2,1280,1728]{1,2,0:T(8,128)(2,1)} %param.16), kind=kOutput, calls=%fused_computation.5 | convolution fusion | flops 4531617792 | bytes 13697024 | tf_op jit(solution)/shard_map/rd,kdf->krf/dot_general | solution.py:403
  52.0 5.8 %copy.84 = bf16[2,512,1728]{2,1,0:T(8,128)(2,1)} copy(bf16[2,512,1728]{1,2,0:T(8,128)(2,1)} %fusion.4) | data formatting | bytes 7077888 | tf_op jit(solution)/shard_map/convert_element_type | solution.py:408
  57.9 40.4 %shard_map.180 = (f32[2,128,1728]{2,1,0:T(8,128)S(1)}, f32[128,1728]{1,0:T(8,128)S(1)}) custom-call(bf16[2,2,2,128,1728]{4,3,2,1,0:T(8,128)(2,1)} %bitcast.117, bf16[2,128,1728]{2,1,0:T(8,128)(2,1)S(1)} %bitcast.111), custom_call_target="tpu_custom_call" | custom-call | tf_op jit(solution)/shard_map/pallas_call | solution.py:80
  98.3 0.4 fusion.12
  98.8 0.6 fusion.19
  99.3 0.4 fusion.16.refs_0_
  99.7 0.3 convolution_multiply_fusion.2.refs_2_
  100.0 32.4 %shard_map.181 = (f32[8,2,128,32]{3,2,1,0:T(8,128)S(1)}, bf16[2,2,128,1728]{3,2,1,0:T(8,128)(2,1)S(1)}, f32[2,2,32,1728]{3,2,1,0:T(8,128)S(1)}) custom-call(f32[2,128,32]{2,1,0:T(8,128)S(1)} %fusion.16.refs_0_, bf16[128,1728]{1,0:T(8,128)(2,1)S(1)} %get-tuple-element.34.refs_1_, f32[2,32,1728]{2,1,0:T(8,128)S(1)} %convolution_multiply_fusion.2.refs_2_), custom_call_target="tpu_custom_call" | custom-call | tf_op jit(solution)/shard_map/pallas_call | solution.py:80
  132.4 0.9 copy-done.1
  133.3 3.6 %fusion.5 = bf16[4,128,1280]{2,1,0:T(8,128)(2,1)} fusion(bf16[4,128,1728]{2,1,0:T(8,128)(2,1)S(1)} %bitcast.114, bf16[1728,1280]{1,0:T(8,128)(2,1)S(1)} %bitcast.125), kind=kOutput, calls=%fused_computation.6 | convolution fusion | flops 2265579520 | bytes 7503872 | tf_op jit(solution)/shard_map/grf,fd->grd/dot_general | solution.py:328
  136.9 3.9 %reshape.62 = bf16[2,2,128,2,640]{4,3,2,1,0:T(2,128)(2,1)} reshape(bf16[4,128,1280]{2,1,0:T(8,128)(2,1)} %fusion.5) | data formatting | bytes 2621440 | tf_op jit(solution)/shard_map/reshape | solution.py:330
  140.8 1.5 copy.92
  142.3 32.6 %shard_map.182 = bf16[128,640]{1,0:T(8,128)(2,1)S(1)} custom-call(bf16[4,2,128,640]{3,2,1,0:T(8,128)(2,1)S(1)} %bitcast.109), custom_call_target="tpu_custom_call" | custom-call | tf_op jit(solution)/shard_map/pallas_call | solution.py:80
  174.9 0.1 reduce_sum.46
  175.0 2.1 reduce_sum.49
  177.1 1.2 fusion.13.refs_0_
  178.3 16.6 %shard_map.183 = f32[2,2,640,32]{3,2,1,0:T(8,128)S(1)} custom-call(f32[2,640,32]{2,1,0:T(8,128)S(1)} %fusion.13.refs_0_), custom_call_target="tpu_custom_call" | custom-call | tf_op jit(solution)/shard_map/pallas_call | solution.py:80
  194.9 1.0 reduce_sum.47
  196.0 1.3 copy.96
  197.3 1.9 fusion.35
  199.2 1.2 convolution_bitcast_fusion.refs_0_
  200.4 19.6 %shard_map.184 = f32[8,2,128,32]{3,2,1,0:T(8,128)S(1)} custom-call(f32[2,128,32]{2,1,0:T(8,128)S(1)} %convolution_bitcast_fusion.refs_0_), custom_call_target="tpu_custom_call" | custom-call | tf_op jit(solution)/shard_map/pallas_call | solution.py:80
  220.0 0.1 reduce_sum.48
  220.2 2.8 fusion.30
  223.0 0.4 fusion.11
  223.5 0.3 copy-done.5
  223.8 0.3 fusion.15.refs_0_
  224.0 16.6 %shard_map.185 = bf16[2,2,128,1728]{3,2,1,0:T(8,128)(2,1)S(1)} custom-call(bf16[128,1728]{1,0:T(8,128)(2,1)S(1)} %fusion.15.refs_0_), custom_call_target="tpu_custom_call" | custom-call | tf_op jit(solution)/shard_map/pallas_call | solution.py:80
  240.7 2.5 fusion.8
  243.3 0.3 reshape.65
  243.6 0.2 copy.103
  243.8 36.5 %shard_map.186 = bf16[128,640]{1,0:T(8,128)(2,1)S(1)} custom-call(bf16[4,2,128,640]{3,2,1,0:T(8,128)(2,1)S(1)} %bitcast.110), custom_call_target="tpu_custom_call" | custom-call | tf_op jit(solution)/shard_map/pallas_call | solution.py:80
  280.3 0.8 select_bitcast_fusion
  (24 shorter events, 0.3 us)
Async XLA Ops:
  32.7 1.0 copy-start
  33.7 1.1 copy-start.2
  36.1 6.1 %copy-start.3 = (bf16[4,128,1280]{2,1,0:T(8,128)(2,1)S(1)}, bf16[4,128,1280]{2,1,0:T(8,128)(2,1)}, u32[]{:S(2)}) copy-start(bf16[4,128,1280]{2,1,0:T(8,128)(2,1)} %copy-done.2) | copy-start | bytes 3932164
  57.9 40.4 %copy-start.4 = (f32[2,32,1728]{2,1,0:T(8,128)S(1)}, f32[2,32,1728]{2,1,0:T(8,128)}, u32[]{:S(2)}) copy-start(f32[2,32,1728]{2,1,0:T(8,128)} %param.19) | copy-start | bytes 1327108
  98.3 35.0 %slice-start = ((s8[4423680]{0:T(1024)(128)(4,1)}), s8[4194304]{0:T(1024)(128)(4,1)S(1)}, s32[]{:S(2)}) async-start(s8[4423680]{0:T(1024)(128)(4,1)} %bitcast.124), calls=%async_computation | async-start | bytes 8388608
  98.7 34.6 %slice-start.1 = ((s8[4423680]{0:T(1024)(128)(4,1)}), s8[229376]{0:T(1024)(128)(4,1)S(1)}, s32[]{:S(2)}) async-start(s8[4423680]{0:T(1024)(128)(4,1)} %bitcast.124), calls=%async_computation.1 | async-start | bytes 458752
  132.4 0.9 copy-start.1
  199.2 23.8 %copy-start.6 = (f32[2,640,32]{1,2,0:T(8,128)}, f32[2,640,32]{1,2,0:T(8,128)S(1)}, u32[]{:S(2)}) copy-start(f32[2,640,32]{1,2,0:T(8,128)S(1)} %get-tuple-element.39) | copy-start | bytes 491524
  220.2 20.5 %slice-start.2 = ((s8[4423680]{0:T(1024)(128)(4,1)}), s8[4194304]{0:T(1024)(128)(4,1)S(1)}, s32[]{:S(2)}) async-start(s8[4423680]{0:T(1024)(128)(4,1)} %bitcast.126), calls=%async_computation.2 | async-start | bytes 8388608
  223.0 0.8 copy-start.5
  223.0 17.7 %slice-start.3 = ((s8[4423680]{0:T(1024)(128)(4,1)}), s8[229376]{0:T(1024)(128)(4,1)S(1)}, s32[]{:S(2)}) async-start(s8[4423680]{0:T(1024)(128)(4,1)} %bitcast.126), calls=%async_computation.3 | async-start | bytes 458752

commit v2 on v1

--- a/solution.py
+++ b/solution.py
@@ -266,8 +266,12 @@
     return call(body, outs, scratch, cid, *operands)
 
 
-def finish_kernel(sizes, part, out, got, summed, far, result, s0, r0, s1, r1, s2, r2):
+def finish_kernel(sizes, with_gather, *refs):
     n_role, n_dp, hidden = sizes
+    if with_gather:
+        part, src, out, dst, got, summed, far, result, s0, r0, s1, r1, s2, r2, s3, r3, s4, r4 = refs
+    else:
+        part, out, got, summed, far, result, s0, r0, s1, r1, s2, r2 = refs
     role, dp, me = (lax.axis_index(a) for a in ("role", "dp", "hidden"))
     pairs = hidden // 2
     pair, odd = me // 2, lax.rem(me, 2)
@@ -277,23 +281,29 @@
     others = [{"hidden": ring(pair, step, pairs) * 2 + odd} for step in range(1, pairs)]
     mate = {"hidden": pair * 2 + 1 - odd}
     barrier = pltpu.get_barrier_semaphore()
-    for peer in others + [mate]:
+    peers = others + [mate]
+    if with_gather:
+        peers = peers + dp_peers(n_dp) + [other_role()]
+    for peer in peers:
         pl.semaphore_signal(barrier, inc=1, device_id=peer, device_id_type=MESH)
 
     @pl.when(mine != pair)
     def _():
         pl.semaphore_signal(barrier, inc=1, device_id=owner, device_id_type=MESH)
 
-    pl.semaphore_wait(barrier, jnp.where(mine != pair, pairs + 1, pairs))
-
-    order = list(range(1, pairs)) + [0]
+    pl.semaphore_wait(barrier, jnp.where(mine != pair, len(peers) + 1, len(peers)))
+
+    if with_gather:
+        over = remote(src, dst.at[dp, role], (s3, r3), 0, other_role())
+        over.start()
     firsts = []
-    for step in order:
+    for step in list(range(1, pairs)) + [0]:
         block = ring(pair, step, pairs)
         copy = remote(part.at[block, 1 - odd], got.at[block], (s0, r0), step, mate)
+        copy.start()
         firsts.append((step, block, copy))
-    for _, _, copy in firsts:
-        copy.start()
+    if with_gather:
+        dst[dp, role] = src[...]
     seconds = []
     for step, block, copy in firsts:
         copy.wait()
@@ -303,6 +313,13 @@
             copy = remote(summed.at[block], far.at[step - 1], (s1, r1), step - 1, others[step - 1])
             copy.start()
             seconds.append(copy)
+    nears = []
+    if with_gather:
+        over.wait()
+        for slot, peer in enumerate(dp_peers(n_dp)):
+            copy = remote(dst.at[dp], dst.at[dp], (s4, r4), slot, peer)
+            copy.start()
+            nears.append(copy)
     total = summed[pair].astype(F32)
     for step, copy in enumerate(seconds):
         copy.wait()
@@ -319,8 +336,11 @@
     def _():
         out[...] = result[...]
 
-
-def finish(sizes, cid, hidden_all, down_weight, live):
+    for copy in nears:
+        copy.wait()
+
+
+def finish(sizes, cid, hidden_all, down_weight, live, gather_in=None):
     n_role, n_dp, hidden = sizes
     rows = hidden_all.shape[2]
     width = down_weight.shape[1]
@@ -331,9 +351,14 @@
     part = part.transpose(1, 0, 3, 2, 4).reshape(n_role * n_dp, per, rows, width // per)
     pairs = hidden // 2
     block = (rows, width // per)
-    (out,) = call(
-        functools.partial(finish_kernel, sizes),
-        [shape_of(block, BF16)],
+    outs, operands, more = [shape_of(block, BF16)], [part], []
+    if gather_in is not None:
+        outs.append(shape_of((n_dp, n_role) + gather_in.shape, gather_in.dtype))
+        operands.append(gather_in)
+        more = dma_pair(1) + dma_pair(n_dp - 1)
+    out, *gathered = call(
+        functools.partial(finish_kernel, sizes, gather_in is not None),
+        outs,
         [
             pltpu.VMEM((pairs,) + block, BF16),
             pltpu.VMEM((pairs,) + block, BF16),
@@ -342,11 +367,12 @@
         ]
         + dma_pair(pairs)
         + dma_pair(pairs - 1)
-        + dma_pair(1),
+        + dma_pair(1)
+        + more,
         cid,
-        part,
-    )
-    return jnp.where(live[:, None], out, jnp.zeros_like(out))
+        *operands,
+    )
+    return [jnp.where(live[:, None], out, jnp.zeros_like(out))] + gathered
 
 
 def local(
@@ -379,7 +405,7 @@
 
     token_part = lax.dynamic_slice_in_dim(token_batch, shard_index * part_width, part_width, 1)
     reduced_part = jnp.einsum(
-        "rd,kdq->krq", token_part, adapter_in.astype(BF16), preferred_element_type=F32
+        "rd,kdq->kqr", token_part, adapter_in.astype(BF16), preferred_element_type=F32
     )
     row_weight = KEEP_RATE ** staleness.astype(F32)
     upstream = (row_weight[:, None] * cotangent.astype(F32)).astype(BF16)
@@ -392,7 +418,7 @@
         [
             shape_of((groups, rows, width), BF16),
             shape_of((n_dp, rows, width), BF16),
-            shape_of((hidden, 2, rows, rank), F32),
+            shape_of((hidden, 2, rank, rows), F32),
         ],
         dma_pair(groups - 1) + dma_pair(n_dp - 1) + dma_pair(hidden - 1),
         1,
@@ -434,7 +460,7 @@
     reduced = reduced_all.sum(axis=0).astype(BF16)
     out_bf = adapter_out.astype(BF16)
     pre = base + ADAPTER_SCALE * jnp.einsum(
-        "krq,kqf->krf", reduced, out_bf, preferred_element_type=F32
+        "kqr,kqf->krf", reduced, out_bf, preferred_element_type=F32
     )
     sigma = jax.nn.sigmoid(pre[0])
     hidden_old = (pre[0] * sigma * pre[1]).astype(BF16)
@@ -442,35 +468,38 @@
     grad_up = (grad_hidden * pre[0] * sigma).astype(BF16)
     grads = jnp.stack([grad_gate, grad_up])
     partial_out = ADAPTER_SCALE * jnp.einsum(
-        "krq,krf->kqf", reduced, grads, preferred_element_type=F32
-    )
-    through_part = jnp.einsum("krf,kqf->krq", grads, out_bf, preferred_element_type=F32)
-    through_all, hidden_old_all, grad_out_all = share(
-        sizes, 3, through_part, hidden_old, partial_out
-    )
+        "kqr,krf->kqf", reduced, grads, preferred_element_type=F32
+    )
+    through_part = jnp.einsum("krf,kqf->kqr", grads, out_bf, preferred_element_type=F32)
+    through_all, hidden_old_all = share(sizes, 3, through_part, hidden_old)
     through = through_all.sum(axis=0).astype(BF16)
     partial_in = ADAPTER_SCALE * jnp.einsum(
-        "un,huj->hnj", token_part, through, preferred_element_type=F32
-    )
-    (grad_in_all,) = share(sizes, 4, None, None, partial_in)
-    grad_in = grad_in_all.sum(axis=0)
+        "un,hju->hjn", token_part, through, preferred_element_type=F32
+    )
+    rank_rows = 2 * rank
+    packed = jnp.concatenate(
+        [partial_in.reshape(rank_rows, -1), partial_out.reshape(rank_rows, -1)], axis=1
+    )
+    (packed_all,) = share(sizes, 4, None, None, packed)
+    grad_in_all = packed_all[:, :, :part_width].reshape(n_dp, 2, rank, part_width)
+    grad_out_all = packed_all[:, :, part_width:].reshape(n_dp, 2, rank, units)
+    grad_in = grad_in_all.sum(axis=0).transpose(0, 2, 1)
     grad_out = grad_out_all.sum(axis=0)
     new_in, new_m_in, new_s_in = adam_update(adapter_in, grad_in, moment_in, square_in, model)
     new_out, new_m_out, new_s_out = adam_update(
         adapter_out, grad_out, moment_out, square_out, model
     )
     new_part = jnp.einsum(
-        "rd,kdq->krq", token_part, new_in.astype(BF16), preferred_element_type=F32
+        "rd,kdq->kqr", token_part, new_in.astype(BF16), preferred_element_type=F32
     )
     (new_all,) = share(sizes, 5, new_part)
     new_reduced = new_all.sum(axis=0).astype(BF16)
     post = base + ADAPTER_SCALE * jnp.einsum(
-        "krq,kqf->krf", new_reduced, new_out.astype(BF16), preferred_element_type=F32
+        "kqr,kqf->krf", new_reduced, new_out.astype(BF16), preferred_element_type=F32
     )
     hidden_new = (jax.nn.silu(post[0]) * post[1]).astype(BF16)
-    (hidden_new_all,) = share(sizes, 6, None, hidden_new)
-    layer_old = finish(sizes, 7, hidden_old_all, down_weight, live)
-    layer_new = finish(sizes, 8, hidden_new_all, down_weight, live)
+    layer_old, hidden_new_all = finish(sizes, 7, hidden_old_all, down_weight, live, hidden_new)
+    (layer_new,) = finish(sizes, 8, hidden_new_all, down_weight, live)
     return (
         layer_old[None],
         layer_new[None],

time: 282 us -> 224 us (0.79)
  Pallas kernels: 217 us -> 166 us
  other arithmetic: 12.8 us -> 5.15 us
  matrix products: 25.6 us -> 28.9 us
  local copies, waits for them, and re-layouts: 24.5 us -> 21.6 us
    pallas_call x8 -> x7, Pallas kernels: 217 us -> 166 us  [call(): pl.pallas_call(body, out_shape=outs, in_specs=[spec] * len(operands), out...]
    dot_general x2, matrix products: 6.14 us -> 10.7 us  [finish(): jnp.einsum('grf,fd->grd', hidden_all.reshape((-1,) + hidden_all.shape[2:]...]
    unnamed x24 -> x32, local copies, waits for them, and re-layouts: 7.52 us -> 9.2 us
where the time goes in v2:
time: 224 us; the launch traced here: 223 us
  Pallas kernels  166 us (74%)
  matrix products  28.9 us (13%)
  local copies, waits for them, and re-layouts  21.6 us (10%)
  other arithmetic  5.15 us (2%)
    pallas_call x7, Pallas kernels, call(): pl.pallas_call(body, out_shape=outs, in_specs=[spec] * len(operands), out...  166 us
    dot_general x2, matrix products, finish(): jnp.einsum('grf,fd->grd', hidden_all.reshape((-1,) + hidden_all.shape[2:]...  10.7 us
    dot_general x1, matrix products, local(): jnp.einsum('rd,kdf->krf', tokens_all.reshape(groups * rows, width), froze...  9.76 us
    unnamed x32, local copies, waits for them, and re-layouts  9.2 us
    convert_element_type x1, local copies, waits for them, and re-layouts, local(): products = jnp.einsum('rd,kdf->krf', tokens_all.reshape(groups * rows, wi...  5.91 us

profile of v2, /device:TPU:1, one launch (start us, length us, event | category | flops | bytes accessed | tf_op | source)
XLA Modules:
  0.0 222.8 jit_solution(11546168548025595476)
XLA Ops:
  0.6 0.9 convert_element_type.60
  1.6 1.1 fusion.23
  2.7 1.8 copy.32
  4.5 0.0 copy-done.14
  4.5 0.3 multiply_convert_fusion
  4.8 0.6 copy.33
  5.4 2.4 %copy.30 = bf16[1,128,5120]{1,2,0:T(8,128)(2,1)} copy(bf16[1,128,5120]{2,1,0:T(8,128)(2,1)} %param.12) | data formatting | bytes 2621440 | tf_op args[0]
  7.8 1.6 copy.31
  9.4 21.6 %shard_map.179 = (bf16[4,128,1280]{2,1,0:T(8,128)(2,1)S(1)}, bf16[2,128,1280]{2,1,0:T(8,128)(2,1)S(1)}, f32[8,2,32,128]{3,2,1,0:T(8,128)S(1)}) custom-call(bf16[4,128,1280]{2,1,0:T(8,128)(2,1)S(1)} %bitcast.113, bf16[4,128,1280]{2,1,0:T(8,128)(2,1)S(1)} %bitcast.112, f32[2,32,128]{2,1,0:T(8,128)S(1)} %bitcast.117), custom_call_target="tpu_custom_call" | custom-call | tf_op jit(solution)/shard_map/pallas_call | solution.py:80
  31.0 0.8 copy-done.4
  31.9 9.8 %fusion.4 = bf16[2,512,1728]{1,2,0:T(8,128)(2,1)} fusion(bf16[512,1280,1]{1,0,2:T(8,128)(2,1)S(1)} %bitcast.120, bf16[2,1280,1728]{1,2,0:T(8,128)(2,1)} %param.16), kind=kOutput, calls=%fused_computation.5 | convolution fusion | flops 4531617792 | bytes 13697024 | tf_op jit(solution)/shard_map/rd,kdf->krf/dot_general | solution.py:429
  41.6 5.9 %copy.34 = bf16[2,512,1728]{2,1,0:T(8,128)(2,1)} copy(bf16[2,512,1728]{1,2,0:T(8,128)(2,1)} %fusion.4) | data formatting | bytes 7077888 | tf_op jit(solution)/shard_map/convert_element_type | solution.py:434
  47.5 3.6 %convolution_convert_fusion.1 = bf16[256,1728]{0,1:T(8,128)(2,1)S(1)} fusion(bf16[256,1280]{1,0:T(8,128)(2,1)S(1)} %bitcast.121, bf16[1728,1280]{1,0:T(8,128)(2,1)} %param.17), kind=kOutput, calls=%fused_computation.13 | convolution fusion | flops 1132904448 | bytes 5963776 | tf_op jit(solution)/shard_map/dot_general | solution.py:435
  51.1 0.6 copy.35
  51.8 0.0 copy-start.6
  51.8 38.8 %shard_map.180 = (f32[2,128,1728]{2,1,0:T(8,128)S(1)}, f32[128,1728]{1,0:T(8,128)S(1)}) custom-call(bf16[2,2,2,128,1728]{4,3,2,1,0:T(8,128)(2,1)} %bitcast.122, bf16[2,128,1728]{2,1,0:T(8,128)(2,1)S(1)} %bitcast.116), custom_call_target="tpu_custom_call" | custom-call | tf_op jit(solution)/shard_map/pallas_call | solution.py:80
  90.6 0.9 copy-done
  91.6 0.4 fusion.12
  92.0 0.7 copy-done.1
  92.7 0.6 fusion.17
  93.4 0.3 convolution_multiply_fusion.2
  93.6 0.4 convolution_bitcast_fusion.refs_0_
  94.0 15.1 %shard_map.181 = (f32[8,2,32,128]{3,2,1,0:T(8,128)S(1)}, bf16[2,2,128,1728]{3,2,1,0:T(8,128)(2,1)S(1)}) custom-call(f32[2,32,128]{2,1,0:T(8,128)S(1)} %convolution_bitcast_fusion.refs_0_, bf16[128,1728]{1,0:T(8,128)(2,1)S(1)} %get-tuple-element.28.refs_1_), custom_call_target="tpu_custom_call" | custom-call | tf_op jit(solution)/shard_map/pallas_call | solution.py:80
  109.2 1.2 copy-done.2
  110.4 1.1 convolution_multiply_fusion.3
  111.5 0.0 copy-start.10
  111.6 0.0 copy-start.11
  111.6 17.2 %shard_map.182 = f32[2,64,2368]{2,1,0:T(8,128)S(1)} custom-call(f32[64,2368]{1,0:T(8,128)S(1)} %pad_maximum_fusion.1.refs_0_), custom_call_target="tpu_custom_call" | custom-call | tf_op jit(solution)/shard_map/pallas_call | solution.py:80
  128.9 0.0 copy-start.9
  128.9 0.0 copy-start.12
  128.9 0.0 copy-start.13
  128.9 1.2 fusion.29
  130.1 0.0 copy-done.9
  130.2 0.8 fusion.34
  131.0 1.1 fusion.20.refs_0_
  132.1 7.5 %shard_map.183 = f32[8,2,32,128]{3,2,1,0:T(8,128)S(1)} custom-call(f32[2,32,128]{2,1,0:T(8,128)S(1)} %fusion.20.refs_0_), custom_call_target="tpu_custom_call" | custom-call | tf_op jit(solution)/shard_map/pallas_call | solution.py:80
  139.7 0.4 fusion.11
  140.2 0.3 fusion.14.refs_1_
  140.4 1.2 copy-done.3
  141.6 5.9 %fusion.5 = bf16[4,128,1280]{2,1,0:T(8,128)(2,1)} fusion(bf16[4,128,1728]{2,1,0:T(8,128)(2,1)S(1)} %bitcast.118, bf16[1728,1280]{1,0:T(8,128)(2,1)} %param.17), kind=kOutput, calls=%fused_computation.6 | convolution fusion | flops 2265579520 | bytes 7503872 | tf_op jit(solution)/shard_map/grf,fd->grd/dot_general | solution.py:348
  147.5 3.0 %reshape.72 = bf16[2,2,128,2,640]{4,3,2,1,0:T(2,128)(2,1)S(1)} reshape(bf16[4,128,1280]{2,1,0:T(8,128)(2,1)} %fusion.5) | data formatting | bytes 2621440 | tf_op jit(solution)/shard_map/reshape | solution.py:350
  150.5 0.2 copy.39
  150.7 36.6 %shard_map.184 = (bf16[128,640]{1,0:T(8,128)(2,1)S(1)}, bf16[2,2,128,1728]{3,2,1,0:T(8,128)(2,1)S(1)}) custom-call(bf16[4,2,128,640]{3,2,1,0:T(8,128)(2,1)S(1)} %bitcast.114, bf16[128,1728]{1,0:T(8,128)(2,1)S(1)} %fusion.14.refs_1_), custom_call_target="tpu_custom_call" | custom-call | tf_op jit(solution)/shard_map/pallas_call | solution.py:80
  187.3 4.8 %fusion.8 = bf16[4,128,1280]{2,1,0:T(8,128)(2,1)S(1)} fusion(bf16[4,128,1728]{2,1,0:T(8,128)(2,1)S(1)} %bitcast.119, bf16[1728,1280]{1,0:T(8,128)(2,1)} %param.17), kind=kOutput, calls=%fused_computation.7 | convolution fusion | flops 2265579520 | bytes 7503872 | tf_op jit(solution)/shard_map/grf,fd->grd/dot_general | solution.py:348
  192.1 0.3 reshape.77
  192.4 0.2 copy.43
  192.6 28.7 %shard_map.185 = bf16[128,640]{1,0:T(8,128)(2,1)S(1)} custom-call(bf16[4,2,128,640]{3,2,1,0:T(8,128)(2,1)S(1)} %bitcast.115), custom_call_target="tpu_custom_call" | custom-call | tf_op jit(solution)/shard_map/pallas_call | solution.py:80
  222.0 0.8 select_bitcast_fusion
  (25 shorter events, 0.2 us)
Async XLA Ops:
  0.6 3.8 %copy-start.14 = (s32[128]{0:T(128)S(1)}, s32[128]{0:T(128)}, u32[]{:S(2)}) copy-start(s32[128]{0:T(128)} %param.14) | copy-start | bytes 1540
  31.0 0.8 copy-start.4
  41.6 5.9 %copy-start.5 = (bf16[2,128,1280]{2,1,0:T(8,128)(2,1)S(1)}, bf16[2,128,1280]{2,1,0:T(8,128)(2,1)}, u32[]{:S(2)}) copy-start(bf16[2,128,1280]{2,1,0:T(8,128)(2,1)} %copy-done.4) | copy-start | bytes 1966084
  51.8 39.8 %copy-start.6 = (f32[2,32,1728]{2,1,0:T(8,128)S(1)}, f32[2,32,1728]{2,1,0:T(8,128)}, u32[]{:S(2)}) copy-start(f32[2,32,1728]{2,1,0:T(8,128)} %param.19) | copy-start | bytes 1327108
  90.6 0.9 copy-start
  91.6 1.2 copy-start.1
  109.2 1.2 copy-start.2
  111.5 17.3 %copy-start.10 = (f32[2,32,1728]{2,1,0:T(8,128)S(1)}, f32[2,32,1728]{2,1,0:T(8,128)}, u32[]{:S(2)}) copy-start(f32[2,32,1728]{2,1,0:T(8,128)} %param.23) | copy-start | bytes 1327108
  111.6 17.3 %copy-start.11 = (f32[2,32,1728]{2,1,0:T(8,128)S(1)}, f32[2,32,1728]{2,1,0:T(8,128)}, u32[]{:S(2)}) copy-start(f32[2,32,1728]{2,1,0:T(8,128)} %param.22) | copy-start | bytes 1327108
  128.9 1.3 copy-start.9
  128.9 1.3 copy-start.12
  128.9 1.3 copy-start.13
  130.1 10.0 %copy-start.7 = (f32[2,32,1728]{2,1,0:T(8,128)}, f32[2,32,1728]{2,1,0:T(8,128)S(1)}, u32[]{:S(2)}) copy-start(f32[2,32,1728]{2,1,0:T(8,128)S(1)} %get-tuple-element.30) | copy-start | bytes 1327108
  131.0 9.1 %copy-start.8 = (f32[2,640,32]{1,2,0:T(8,128)}, f32[2,640,32]{1,2,0:T(8,128)S(1)}, u32[]{:S(2)}) copy-start(f32[2,640,32]{1,2,0:T(8,128)S(1)} %get-tuple-element.33) | copy-start | bytes 491524
  140.1 1.5 copy-start.3

commit v3 on v2

--- a/solution.py
+++ b/solution.py
@@ -75,12 +75,13 @@
     return {"role": 1 - lax.axis_index("role")}
 
 
-def call(body, outs, scratch, cid, *operands):
+def call(body, outs, scratch, cid, *operands, anywhere=0):
     spec = pl.BlockSpec(memory_space=pltpu.VMEM)
     return pl.pallas_call(
         body,
         out_shape=outs,
-        in_specs=[spec] * len(operands),
+        in_specs=[spec] * (len(operands) - anywhere)
+        + [pl.BlockSpec(memory_space=pl.ANY)] * anywhere,
         out_specs=[spec] * len(outs),
         scratch_shapes=scratch,
         compiler_params=pltpu.CompilerParams(
@@ -104,7 +105,7 @@
     ]
     greet([{"role": a, "dp": b} for a, b in group] + hidden_peers(hidden))
     copies = []
-    own = dp * n_role + role
+    own = role * n_dp + dp
     for slot, (a, b) in enumerate(group):
         copies.append(
             remote(tok.at[a * n_dp + b], tok_all.at[own], (s0, r0), slot, {"role": a, "dp": b})
@@ -122,67 +123,109 @@
         copy.wait()
 
 
-def reduce_kernel(sizes, part, grad, base, grad_sum, got, got_grad, out_part, out_grad, far, far_grad,
-                  s0, r0, s1, r1, s2, r2, s3, r3):
+def product_kernel(sizes, tok, up, weight, down, base, grad_sum, held, held_down, theirs, ours, grads,
+                   got_theirs, got_ours, got_grads, out_part, out_grad, far, far_grad, load,
+                   s0, r0, s1, r1, s2, r2, s3, r3, s4, r4):
     n_role, n_dp, _ = sizes
     role, dp = lax.axis_index("role"), lax.axis_index("dp")
-    greet(dp_peers(n_dp) + [other_role()])
-    copies = []
-    for slot, peer in enumerate(dp_peers(n_dp)):
-        copies.append(remote(part.at[:, peer["dp"]], got.at[slot], (s0, r0), slot, peer))
-        copies.append(remote(grad.at[peer["dp"]], got_grad.at[slot], (s1, r1), slot, peer))
-    for copy in copies:
+    rows, width = tok.shape[2], tok.shape[3]
+    units = weight.shape[2]
+    mates = dp_peers(n_dp)
+    loads = [pltpu.make_async_copy(weight.at[k], held.at[k], load.at[k]) for k in range(2)]
+    loads.append(pltpu.make_async_copy(down, held_down, load.at[2]))
+    for copy in loads:
         copy.start()
-    for copy in copies:
-        copy.wait()
-    rows = base.shape[1]
-    step = 16
-
-    @pl.loop(0, rows // step)
-    def _(i):
-        at = pl.ds(pl.multiple_of(i * step, step), step)
-        for k in range(2):
-            total = part[k, dp, 1 - role, at].astype(F32)
-            for slot in range(n_dp - 1):
-                total = total + got[slot, k, 1 - role, at].astype(F32)
-            out_part[k, at] = total.astype(BF16)
-        total = grad[dp, at].astype(F32)
+    greet(mates + [other_role()])
+
+    def product(which, k):
+        left = tok[which].reshape(n_dp * rows, width)
+        value = jnp.dot(left, held[k], preferred_element_type=F32)
+        return value.astype(BF16).reshape(n_dp, rows, units)
+
+    def send(src, dst, pair, first):
+        copies = [
+            remote(src.at[peer["dp"]], dst.at[slot], pair, first + slot, peer)
+            for slot, peer in enumerate(mates)
+        ]
+        for copy in copies:
+            copy.start()
+        return copies
+
+    def settle(copies, add):
+        for copy in copies:
+            copy.wait()
+        step = 16
+
+        @pl.loop(0, rows // step)
+        def _(i):
+            add(pl.ds(pl.multiple_of(i * step, step), step))
+
+    def summed(mine, got, at):
+        total = mine[dp, at].astype(F32)
         for slot in range(n_dp - 1):
-            total = total + got_grad[slot, at].astype(F32)
-        out_grad[at] = total.astype(BF16)
-
-    across = remote(out_part, far, (s2, r2), 0, other_role())
+            total = total + got[slot, at].astype(F32)
+        return total
+
+    sent = []
+    for k in range(2):
+        loads[k].wait()
+        theirs[k] = product(1 - role, k)
+        sent.append(send(theirs.at[k], got_theirs.at[k], (s0, r0), k * (n_dp - 1)))
+    across = []
+    for k in range(2):
+
+        def add(at, k=k):
+            out_part[k, at] = summed(theirs.at[k], got_theirs.at[k], at).astype(BF16)
+
+        settle(sent[k], add)
+        across.append(remote(out_part.at[k], far.at[k], (s2, r2), k, other_role()))
+        across[k].start()
+    loads[2].wait()
+    value = lax.dot_general(
+        up[...].reshape(n_dp * rows, width),
+        held_down[...],
+        (((1,), (1,)), ((), ())),
+        preferred_element_type=F32,
+    )
+    grads[...] = value.astype(BF16).reshape(n_dp, rows, units)
+    sent_grad = send(grads, got_grads, (s1, r1), 0)
+    sent = []
+    for k in range(2):
+        ours[k] = product(role, k)
+        sent.append(send(ours.at[k], got_ours.at[k], (s4, r4), k * (n_dp - 1)))
+
+    def add_grad(at):
+        out_grad[at] = summed(grads, got_grads, at).astype(BF16)
+
+    settle(sent_grad, add_grad)
     across_grad = remote(out_grad, far_grad, (s3, r3), 0, other_role())
-    across.start()
 
     @pl.when(role == 1)
     def _():
         across_grad.start()
+
+    for k in range(2):
+
+        def add_own(at, k=k):
+            base[k, at] = summed(ours.at[k], got_ours.at[k], at)
+
+        settle(sent[k], add_own)
+    for k in range(2):
+
+        def add_far(at, k=k):
+            base[k, at] = base[k, at] + far[k, at].astype(F32)
+
+        settle([across[k]], add_far)
+
+    @pl.when(role == 1)
+    def _():
         across_grad.wait_send()
+        grad_sum[...] = jnp.zeros_like(grad_sum)
 
     @pl.when(role == 0)
     def _():
         across_grad.wait_recv()
-
-    across.wait()
-    keep = jnp.where(role == 0, 1.0, 0.0).astype(F32)
-
-    @pl.loop(0, rows // step)
-    def _(i):
-        at = pl.ds(pl.multiple_of(i * step, step), step)
-        for k in range(2):
-            total = part[k, dp, role, at].astype(F32)
-            for slot in range(n_dp - 1):
-                total = total + got[slot, k, role, at].astype(F32)
-            base[k, at] = total + far[k, at].astype(F32)
-
-        @pl.when(role == 0)
-        def _():
-            grad_sum[at] = out_grad[at].astype(F32) + far_grad[at].astype(F32)
-
-        @pl.when(role == 1)
-        def _():
-            grad_sum[at] = jnp.zeros_like(grad_sum[at])
+        grad_sum[...] = out_grad[...].astype(F32) + far_grad[...].astype(F32)
 
 
 def share_kernel(sizes, with_hidden, with_gather, with_grad, *refs):
@@ -426,36 +469,37 @@
         blocked(upstream),
         reduced_part,
     )
-    products = jnp.einsum(
-        "rd,kdf->krf",
-        tokens_all.reshape(groups * rows, width),
+    sum_shape = (rows, units)
+    mates = n_dp - 1
+    base, grad_hidden = call(
+        functools.partial(product_kernel, sizes),
+        [shape_of((2,) + sum_shape, F32), shape_of(sum_shape, F32)],
+        [
+            pltpu.VMEM((2, width, units), BF16),
+            pltpu.VMEM((units, width), BF16),
+            pltpu.VMEM((2, n_dp) + sum_shape, BF16),
+            pltpu.VMEM((2, n_dp) + sum_shape, BF16),
+            pltpu.VMEM((n_dp,) + sum_shape, BF16),
+            pltpu.VMEM((2, mates) + sum_shape, BF16),
+            pltpu.VMEM((2, mates) + sum_shape, BF16),
+            pltpu.VMEM((mates,) + sum_shape, BF16),
+            pltpu.VMEM((2,) + sum_shape, BF16),
+            pltpu.VMEM(sum_shape, BF16),
+            pltpu.VMEM((2,) + sum_shape, BF16),
+            pltpu.VMEM(sum_shape, BF16),
+            pltpu.SemaphoreType.DMA((3,)),
+        ]
+        + dma_pair(2 * mates)
+        + dma_pair(mates)
+        + dma_pair(2)
+        + dma_pair(1)
+        + dma_pair(2 * mates),
+        2,
+        tokens_all.reshape(n_role, n_dp, rows, width),
+        upstream_all,
         frozen_gate_up_weight,
-        preferred_element_type=F32,
-    ).astype(BF16).reshape(2, n_dp, n_role, rows, units)
-    grad_products = lax.dot_general(
-        upstream_all.reshape(n_dp * rows, width),
         down_weight,
-        (((1,), (1,)), ((), ())),
-        preferred_element_type=F32,
-    ).astype(BF16).reshape(n_dp, rows, units)
-    base, grad_hidden = call(
-        functools.partial(reduce_kernel, sizes),
-        [shape_of((2, rows, units), F32), shape_of((rows, units), F32)],
-        [
-            pltpu.VMEM((n_dp - 1, 2, n_role, rows, units), BF16),
-            pltpu.VMEM((n_dp - 1, rows, units), BF16),
-            pltpu.VMEM((2, rows, units), BF16),
-            pltpu.VMEM((rows, units), BF16),
-            pltpu.VMEM((2, rows, units), BF16),
-            pltpu.VMEM((rows, units), BF16),
-        ]
-        + dma_pair(n_dp - 1)
-        + dma_pair(n_dp - 1)
-        + dma_pair(1)
-        + dma_pair(1),
-        2,
-        products,
-        grad_products,
+        anywhere=2,
     )
     reduced = reduced_all.sum(axis=0).astype(BF16)
     out_bf = adapter_out.astype(BF16)

time: 224 us -> 211 us (0.942)
  matrix products: 28.9 us -> 10.7 us
  local copies, waits for them, and re-layouts: 21.6 us -> 26.5 us
  other arithmetic: 5.15 us -> 9.11 us
  Pallas kernels: 166 us -> 163 us
    dot_general x2 -> x0, matrix products: 13.4 us -> none  [the longest x1 9.76 us: local(): jnp.einsum('rd,kdf->krf', tokens_all.reshape(groups * rows, width), froze...]
    unnamed x32 -> x31, local copies, waits for them, and re-layouts: 9.2 us -> 21 us
    convert_element_type x2 -> x0, local copies, waits for them, and re-layouts: 6.52 us -> none  [the longest x1 5.91 us: local(): products = jnp.einsum('rd,kdf->krf', tokens_all.reshape(groups * rows, wi...]
    dot_general x2, matrix products: 10.7 us -> 5.07 us  [finish(): jnp.einsum('grf,fd->grd', hidden_all.reshape((-1,) + hidden_all.shape[2:]...]
    pallas_call x7, Pallas kernels: 166 us -> 163 us  [call(): pl.pallas_call(body, out_shape=outs, in_specs=[spec] * (len(operands) - a...]
where the time goes in v3:
time: 211 us
  Pallas kernels  163 us (77%)
  local copies, waits for them, and re-layouts  26.5 us (13%)
  matrix products  10.7 us (5%)
  other arithmetic  9.11 us (4%)
    pallas_call x7, Pallas kernels, call(): pl.pallas_call(body, out_shape=outs, in_specs=[spec] * (len(operands) - a...  163 us
    unnamed x31, local copies, waits for them, and re-layouts  21 us
    dot_general x2, matrix products, finish(): jnp.einsum('grf,fd->grd', hidden_all.reshape((-1,) + hidden_all.shape[2:]...  5.07 us

profile of v3, /device:TPU:1, one launch (start us, length us, event | category | flops | bytes accessed | tf_op | source)
XLA Modules:
  0.0 210.6 jit_solution(16760450143114588389)
XLA Ops:
  1.3 0.7 convert_power_fusion
  2.0 0.9 convert_element_type.51
  2.9 1.1 fusion.22
  4.0 1.8 copy.31
  5.8 0.3 multiply_convert_fusion
  6.0 0.6 copy.32
  6.7 2.4 %copy.29 = bf16[1,128,5120]{1,2,0:T(8,128)(2,1)} copy(bf16[1,128,5120]{2,1,0:T(8,128)(2,1)} %param.12) | data formatting | bytes 2621440 | tf_op args[0]
  9.1 1.6 copy.30
  10.7 21.6 %shard_map.179 = (bf16[4,128,1280]{2,1,0:T(8,128)(2,1)S(1)}, bf16[2,128,1280]{2,1,0:T(8,128)(2,1)S(1)}, f32[8,2,32,128]{3,2,1,0:T(8,128)S(1)}) custom-call(bf16[4,128,1280]{2,1,0:T(8,128)(2,1)S(1)} %bitcast.103, bf16[4,128,1280]{2,1,0:T(8,128)(2,1)S(1)} %bitcast.102, f32[2,32,128]{2,1,0:T(8,128)S(1)} %bitcast.106), custom_call_target="tpu_custom_call" | custom-call | tf_op jit(solution)/shard_map/pallas_call | solution.py:80
  32.3 0.0 copy-start
  32.3 1.0 copy-done
  33.4 0.8 copy-done.2
  34.2 12.8 %copy.33.weight = bf16[2,1280,1728]{2,1,0:T(8,128)(2,1)} copy(bf16[2,1280,1728]{1,2,0:T(8,128)(2,1)} %param.16) | data formatting | bytes 17694720 | tf_op args[4]
  47.1 1.1 copy-done.3
  48.1 36.3 %shard_map.180 = (f32[2,128,1728]{2,1,0:T(8,128)S(1)}, f32[128,1728]{1,0:T(8,128)S(1)}) custom-call(bf16[2,2,128,1280]{3,2,1,0:T(8,128)(2,1)S(1)} %bitcast.105, bf16[2,128,1280]{2,1,0:T(8,128)(2,1)S(1)} %copy-done.3, bf16[2,1280,1728]{2,1,0:T(8,128)(2,1)} %copy.33.weight, bf16[1728,1280]{1,0:T(8,128)(2,1)} %down.1), custom_call_target="tpu_custom_call" | custom-call | tf_op jit(solution)/shard_map/pallas_call | solution.py:80
  84.4 0.0 slice-start
  84.5 0.4 fusion.11
  84.9 0.0 slice-start.1
  84.9 0.6 fusion.16
  85.5 0.4 convolution_bitcast_fusion.refs_0_
  85.9 1.1 convolution_multiply_fusion.2
  87.0 15.1 %shard_map.181 = (f32[8,2,32,128]{3,2,1,0:T(8,128)S(1)}, bf16[2,2,128,1728]{3,2,1,0:T(8,128)(2,1)S(1)}) custom-call(f32[2,32,128]{2,1,0:T(8,128)S(1)} %convolution_bitcast_fusion.refs_0_, bf16[128,1728]{1,0:T(8,128)(2,1)S(1)} %get-tuple-element.28.refs_1_), custom_call_target="tpu_custom_call" | custom-call | tf_op jit(solution)/shard_map/pallas_call | solution.py:80
  102.0 0.0 slice-done
  102.1 2.5 %fusion.4 = bf16[4,128,1280]{2,1,0:T(8,128)(2,1)S(1)} fusion(bf16[4,128,1728]{2,1,0:T(8,128)(2,1)S(1)} %bitcast.107, bf16[1728,1280]{1,0:T(8,128)(2,1)S(1)} %bitcast.112), kind=kOutput, calls=%fused_computation.4 | convolution fusion | flops 2265579520 | bytes 7503872 | tf_op jit(solution)/shard_map/grf,fd->grd/dot_general | solution.py:391
  104.6 1.3 reshape.60
  105.9 1.5 copy.37
  107.4 1.1 convolution_multiply_fusion.3
  108.5 1.1 pad_maximum_fusion.1.refs_0_
  109.5 0.0 copy-start.7
  109.5 0.0 copy-start.8
  109.5 0.0 copy-start.9
  109.6 17.7 %shard_map.182 = f32[2,64,2368]{2,1,0:T(8,128)S(1)} custom-call(f32[64,2368]{1,0:T(8,128)S(1)} %pad_maximum_fusion.1.refs_0_), custom_call_target="tpu_custom_call" | custom-call | tf_op jit(solution)/shard_map/pallas_call | solution.py:80
  127.3 0.8 slice_reduce_fusion
  128.1 0.8 fusion.33
  128.9 0.7 copy-done.6
  129.6 1.1 fusion.19.refs_0_
  130.6 6.8 %shard_map.183 = f32[8,2,32,128]{3,2,1,0:T(8,128)S(1)} custom-call(f32[2,32,128]{2,1,0:T(8,128)S(1)} %fusion.19.refs_0_), custom_call_target="tpu_custom_call" | custom-call | tf_op jit(solution)/shard_map/pallas_call | solution.py:80
  137.4 0.0 slice-start.2
  137.5 2.8 %fusion.28 = (f32[1,2,32,1728]{3,2,1,0:T(8,128)}, f32[2,32,1728]{2,1,0:T(8,128)S(1)}, f32[1,2,32,1728]{3,2,1,0:T(8,128)}) fusion(f32[2,32,1728]{2,1,0:T(8,128)} %bitcast.116, f32[2,32,1728]{2,1,0:T(8,128)} %param.23, f32[2,32,1728]{2,1,0:T(8,128)} %param.19, f32[2,32,1728]{2,1,0:T(8,128)} %param.22), kind=kLoop, calls=%fused_computation.50 | loop fusion | flops 1327104 | bytes 3096576 | tf_op jit(solution)/shard_map/broadcast_in_dim | solution.py:555
  140.3 0.4 fusion.10
  140.7 0.3 copy-done.5
  141.0 0.3 fusion.13.refs_1_
  141.3 35.1 %shard_map.184 = (bf16[128,640]{1,0:T(8,128)(2,1)S(1)}, bf16[2,2,128,1728]{3,2,1,0:T(8,128)(2,1)S(1)}) custom-call(bf16[4,2,128,640]{3,2,1,0:T(8,128)(2,1)S(1)} %bitcast.101, bf16[128,1728]{1,0:T(8,128)(2,1)S(1)} %fusion.13.refs_1_), custom_call_target="tpu_custom_call" | custom-call | tf_op jit(solution)/shard_map/pallas_call | solution.py:80
  176.4 2.5 %fusion.7 = bf16[4,128,1280]{2,1,0:T(8,128)(2,1)S(1)} fusion(bf16[4,128,1728]{2,1,0:T(8,128)(2,1)S(1)} %bitcast.108, bf16[1728,1280]{1,0:T(8,128)(2,1)S(1)} %bitcast.114), kind=kOutput, calls=%fused_computation.5 | convolution fusion | flops 2265579520 | bytes 7503872 | tf_op jit(solution)/shard_map/grf,fd->grd/dot_general | solution.py:391
  178.9 0.3 reshape.65
  179.3 0.2 copy.41
  179.4 30.3 %shard_map.185 = bf16[128,640]{1,0:T(8,128)(2,1)S(1)} custom-call(bf16[4,2,128,640]{3,2,1,0:T(8,128)(2,1)S(1)} %bitcast.104), custom_call_target="tpu_custom_call" | custom-call | tf_op jit(solution)/shard_map/pallas_call | solution.py:80
  209.7 0.8 select_bitcast_fusion
  (22 shorter events, 0.1 us)
Async XLA Ops:
  32.3 1.0 copy-start
  33.4 0.8 copy-start.2
  34.2 12.8 %copy-start.1 = (bf16[4,128,1280]{2,1,0:T(8,128)(2,1)S(1)}, bf16[4,128,1280]{2,1,0:T(8,128)(2,1)}, u32[]{:S(2)}) copy-start(bf16[4,128,1280]{2,1,0:T(8,128)(2,1)} %copy-done) | copy-start | bytes 3932164
  47.1 1.1 copy-start.3
  48.1 36.3 %copy-start.4 = (f32[2,32,1728]{2,1,0:T(8,128)S(1)}, f32[2,32,1728]{2,1,0:T(8,128)}, u32[]{:S(2)}) copy-start(f32[2,32,1728]{2,1,0:T(8,128)} %param.19) | copy-start | bytes 1327108
  84.4 17.6 %slice-start = ((s8[4423680]{0:T(1024)(128)(4,1)}), s8[4194304]{0:T(1024)(128)(4,1)S(1)}, s32[]{:S(2)}) async-start(s8[4423680]{0:T(1024)(128)(4,1)} %bitcast.111), calls=%async_computation | async-start | bytes 8388608
  84.9 17.1 %slice-start.1 = ((s8[4423680]{0:T(1024)(128)(4,1)}), s8[229376]{0:T(1024)(128)(4,1)S(1)}, s32[]{:S(2)}) async-start(s8[4423680]{0:T(1024)(128)(4,1)} %bitcast.111), calls=%async_computation.1 | async-start | bytes 458752
  109.5 18.6 %copy-start.7 = (f32[2,640,32]{1,2,0:T(8,128)S(1)}, f32[2,640,32]{1,2,0:T(8,128)}, u32[]{:S(2)}) copy-start(f32[2,640,32]{1,2,0:T(8,128)} %param.18) | copy-start | bytes 491524
  109.5 18.5 %copy-start.8 = (f32[2,640,32]{1,2,0:T(8,128)S(1)}, f32[2,640,32]{1,2,0:T(8,128)}, u32[]{:S(2)}) copy-start(f32[2,640,32]{1,2,0:T(8,128)} %param.21) | copy-start | bytes 491524
  109.5 18.5 %copy-start.9 = (f32[2,640,32]{1,2,0:T(8,128)S(1)}, f32[2,640,32]{1,2,0:T(8,128)}, u32[]{:S(2)}) copy-start(f32[2,640,32]{1,2,0:T(8,128)} %param.20) | copy-start | bytes 491524
  128.9 0.7 copy-start.6
  137.4 38.9 %slice-start.2 = ((s8[4423680]{0:T(1024)(128)(4,1)}), s8[4194304]{0:T(1024)(128)(4,1)S(1)}, s32[]{:S(2)}) async-start(s8[4423680]{0:T(1024)(128)(4,1)} %bitcast.113), calls=%async_computation.2 | async-start | bytes 8388608
  140.3 0.8 copy-start.5
  140.3 36.1 %slice-start.3 = ((s8[4423680]{0:T(1024)(128)(4,1)}), s8[229376]{0:T(1024)(128)(4,1)S(1)}, s32[]{:S(2)}) async-start(s8[4423680]{0:T(1024)(128)(4,1)} %bitcast.113), calls=%async_computation.3 | async-start | bytes 458752

commit v4 on v3

--- a/solution.py
+++ b/solution.py
@@ -129,7 +129,7 @@
     n_role, n_dp, _ = sizes
     role, dp = lax.axis_index("role"), lax.axis_index("dp")
     rows, width = tok.shape[2], tok.shape[3]
-    units = weight.shape[2]
+    units = weight.shape[1]
     mates = dp_peers(n_dp)
     loads = [pltpu.make_async_copy(weight.at[k], held.at[k], load.at[k]) for k in range(2)]
     loads.append(pltpu.make_async_copy(down, held_down, load.at[2]))
@@ -139,7 +139,9 @@
 
     def product(which, k):
         left = tok[which].reshape(n_dp * rows, width)
-        value = jnp.dot(left, held[k], preferred_element_type=F32)
+        value = lax.dot_general(
+            left, held[k], (((1,), (1,)), ((), ())), preferred_element_type=F32
+        )
         return value.astype(BF16).reshape(n_dp, rows, units)
 
     def send(src, dst, pair, first):
@@ -475,7 +477,7 @@
         functools.partial(product_kernel, sizes),
         [shape_of((2,) + sum_shape, F32), shape_of(sum_shape, F32)],
         [
-            pltpu.VMEM((2, width, units), BF16),
+            pltpu.VMEM((2, units, width), BF16),
             pltpu.VMEM((units, width), BF16),
             pltpu.VMEM((2, n_dp) + sum_shape, BF16),
             pltpu.VMEM((2, n_dp) + sum_shape, BF16),
@@ -497,7 +499,7 @@
         2,
         tokens_all.reshape(n_role, n_dp, rows, width),
         upstream_all,
-        frozen_gate_up_weight,
+        frozen_gate_up_weight.transpose(0, 2, 1),
         down_weight,
         anywhere=2,
     )

time: 211 us -> 199 us (0.943)
  local copies, waits for them, and re-layouts: 26.5 us -> 13.8 us
    unnamed x31 -> x28, local copies, waits for them, and re-layouts: 21 us -> 8.39 us
where the time goes in v4:
time: 199 us
  Pallas kernels  163 us (82%)
  local copies, waits for them, and re-layouts  13.8 us (7%)
  matrix products  11.3 us (6%)
  other arithmetic  9.11 us (5%)
    pallas_call x7, Pallas kernels, call(): pl.pallas_call(body, out_shape=outs, in_specs=[spec] * (len(operands) - a...  163 us
    unnamed x28, local copies, waits for them, and re-layouts  8.39 us
    dot_general x2, matrix products, finish(): jnp.einsum('grf,fd->grd', hidden_all.reshape((-1,) + hidden_all.shape[2:]...  5.07 us

profile of v4, /device:TPU:1, one launch (start us, length us, event | category | flops | bytes accessed | tf_op | source)
XLA Modules:
  0.0 198.5 jit_solution(16459017533192214417)
XLA Ops:
  1.3 0.7 convert_power_fusion
  2.0 0.9 convert_element_type.51
  2.9 1.7 fusion.22
  4.6 1.8 copy.30
  6.4 0.3 multiply_convert_fusion
  6.7 0.6 copy.31
  7.3 2.4 %copy.28 = bf16[1,128,5120]{1,2,0:T(8,128)(2,1)} copy(bf16[1,128,5120]{2,1,0:T(8,128)(2,1)} %param.12) | data formatting | bytes 2621440 | tf_op args[0]
  9.7 1.6 copy.29
  11.3 0.0 copy-start.2
  11.4 0.7 copy-done.2
  12.1 21.5 %shard_map.179 = (bf16[4,128,1280]{2,1,0:T(8,128)(2,1)S(1)}, bf16[2,128,1280]{2,1,0:T(8,128)(2,1)S(1)}, f32[8,2,32,128]{3,2,1,0:T(8,128)S(1)}) custom-call(bf16[4,128,1280]{2,1,0:T(8,128)(2,1)S(1)} %bitcast.104, bf16[4,128,1280]{2,1,0:T(8,128)(2,1)S(1)} %bitcast.103, f32[2,32,128]{2,1,0:T(8,128)S(1)} %bitcast.107), custom_call_target="tpu_custom_call" | custom-call | tf_op jit(solution)/shard_map/pallas_call | solution.py:80
  33.6 0.0 copy-start
  33.7 1.1 copy-done
  34.8 0.0 copy-start.1
  34.8 1.3 copy-done.1
  36.1 36.3 %shard_map.180 = (f32[2,128,1728]{2,1,0:T(8,128)S(1)}, f32[128,1728]{1,0:T(8,128)S(1)}) custom-call(bf16[2,2,128,1280]{3,2,1,0:T(8,128)(2,1)S(1)} %bitcast.106, bf16[2,128,1280]{2,1,0:T(8,128)(2,1)S(1)} %get-tuple-element.18.up, bf16[2,1728,1280]{2,1,0:T(8,128)(2,1)} %bitcast.110, bf16[1728,1280]{1,0:T(8,128)(2,1)} %down.1), custom_call_target="tpu_custom_call" | custom-call | tf_op jit(solution)/shard_map/pallas_call | solution.py:80
  72.4 0.0 slice-start
  72.4 0.4 fusion.11
  72.9 0.0 slice-start.1
  72.9 0.6 fusion.16
  73.5 0.4 convolution_bitcast_fusion.refs_0_
  73.9 1.1 convolution_multiply_fusion.2
  74.9 15.1 %shard_map.181 = (f32[8,2,32,128]{3,2,1,0:T(8,128)S(1)}, bf16[2,2,128,1728]{3,2,1,0:T(8,128)(2,1)S(1)}) custom-call(f32[2,32,128]{2,1,0:T(8,128)S(1)} %convolution_bitcast_fusion.refs_0_, bf16[128,1728]{1,0:T(8,128)(2,1)S(1)} %get-tuple-element.28.refs_1_), custom_call_target="tpu_custom_call" | custom-call | tf_op jit(solution)/shard_map/pallas_call | solution.py:80
  90.0 2.5 %fusion.4 = bf16[4,128,1280]{2,1,0:T(8,128)(2,1)S(1)} fusion(bf16[4,128,1728]{2,1,0:T(8,128)(2,1)S(1)} %bitcast.108, bf16[1728,1280]{1,0:T(8,128)(2,1)S(1)} %bitcast.114), kind=kOutput, calls=%fused_computation.4 | convolution fusion | flops 2265579520 | bytes 7503872 | tf_op jit(solution)/shard_map/grf,fd->grd/dot_general | solution.py:393
  92.6 1.3 reshape.60
  93.9 1.5 copy.35
  95.4 1.1 convolution_multiply_fusion.3
  96.4 1.1 pad_maximum_fusion.1.refs_0_
  97.5 0.0 copy-start.6
  97.5 0.0 copy-start.7
  97.5 0.0 copy-start.8
  97.6 17.7 %shard_map.182 = f32[2,64,2368]{2,1,0:T(8,128)S(1)} custom-call(f32[64,2368]{1,0:T(8,128)S(1)} %pad_maximum_fusion.1.refs_0_), custom_call_target="tpu_custom_call" | custom-call | tf_op jit(solution)/shard_map/pallas_call | solution.py:80
  115.3 0.8 slice_reduce_fusion
  116.1 0.8 fusion.33
  116.9 0.7 copy-done.5
  117.6 1.1 fusion.19.refs_0_
  118.6 6.8 %shard_map.183 = f32[8,2,32,128]{3,2,1,0:T(8,128)S(1)} custom-call(f32[2,32,128]{2,1,0:T(8,128)S(1)} %fusion.19.refs_0_), custom_call_target="tpu_custom_call" | custom-call | tf_op jit(solution)/shard_map/pallas_call | solution.py:80
  125.4 0.0 slice-start.2
  125.5 2.8 %fusion.28 = (f32[1,2,32,1728]{3,2,1,0:T(8,128)}, f32[2,32,1728]{2,1,0:T(8,128)S(1)}, f32[1,2,32,1728]{3,2,1,0:T(8,128)}) fusion(f32[2,32,1728]{2,1,0:T(8,128)} %bitcast.118, f32[2,32,1728]{2,1,0:T(8,128)} %param.23, f32[2,32,1728]{2,1,0:T(8,128)} %param.19, f32[2,32,1728]{2,1,0:T(8,128)} %param.22), kind=kLoop, calls=%fused_computation.50 | loop fusion | flops 1327104 | bytes 3096576 | tf_op jit(solution)/shard_map/broadcast_in_dim | solution.py:557
  128.3 0.4 fusion.10
  128.7 0.3 copy-done.4
  129.0 0.3 fusion.13.refs_1_
  129.3 35.1 %shard_map.184 = (bf16[128,640]{1,0:T(8,128)(2,1)S(1)}, bf16[2,2,128,1728]{3,2,1,0:T(8,128)(2,1)S(1)}) custom-call(bf16[4,2,128,640]{3,2,1,0:T(8,128)(2,1)S(1)} %bitcast.102, bf16[128,1728]{1,0:T(8,128)(2,1)S(1)} %fusion.13.refs_1_), custom_call_target="tpu_custom_call" | custom-call | tf_op jit(solution)/shard_map/pallas_call | solution.py:80
  164.4 2.5 %fusion.7 = bf16[4,128,1280]{2,1,0:T(8,128)(2,1)S(1)} fusion(bf16[4,128,1728]{2,1,0:T(8,128)(2,1)S(1)} %bitcast.109, bf16[1728,1280]{1,0:T(8,128)(2,1)S(1)} %bitcast.116), kind=kOutput, calls=%fused_computation.5 | convolution fusion | flops 2265579520 | bytes 7503872 | tf_op jit(solution)/shard_map/grf,fd->grd/dot_general | solution.py:393
  166.9 0.3 reshape.65
  167.3 0.2 copy.39
  167.4 30.3 %shard_map.185 = bf16[128,640]{1,0:T(8,128)(2,1)S(1)} custom-call(bf16[4,2,128,640]{3,2,1,0:T(8,128)(2,1)S(1)} %bitcast.105), custom_call_target="tpu_custom_call" | custom-call | tf_op jit(solution)/shard_map/pallas_call | solution.py:80
  197.7 0.8 select_bitcast_fusion
  (19 shorter events, 0.1 us)
Async XLA Ops:
  11.3 0.8 copy-start.2
  33.6 1.1 copy-start
  34.8 1.3 copy-start.1
  36.1 36.3 %copy-start.3 = (f32[2,32,1728]{2,1,0:T(8,128)S(1)}, f32[2,32,1728]{2,1,0:T(8,128)}, u32[]{:S(2)}) copy-start(f32[2,32,1728]{2,1,0:T(8,128)} %param.19) | copy-start | bytes 1327108
  72.4 17.6 %slice-start = ((s8[4423680]{0:T(1024)(128)(4,1)}), s8[4194304]{0:T(1024)(128)(4,1)S(1)}, s32[]{:S(2)}) async-start(s8[4423680]{0:T(1024)(128)(4,1)} %bitcast.113), calls=%async_computation | async-start | bytes 8388608
  72.9 17.1 %slice-start.1 = ((s8[4423680]{0:T(1024)(128)(4,1)}), s8[229376]{0:T(1024)(128)(4,1)S(1)}, s32[]{:S(2)}) async-start(s8[4423680]{0:T(1024)(128)(4,1)} %bitcast.113), calls=%async_computation.1 | async-start | bytes 458752
  97.5 18.6 %copy-start.6 = (f32[2,640,32]{1,2,0:T(8,128)S(1)}, f32[2,640,32]{1,2,0:T(8,128)}, u32[]{:S(2)}) copy-start(f32[2,640,32]{1,2,0:T(8,128)} %param.18) | copy-start | bytes 491524
  97.5 18.5 %copy-start.7 = (f32[2,640,32]{1,2,0:T(8,128)S(1)}, f32[2,640,32]{1,2,0:T(8,128)}, u32[]{:S(2)}) copy-start(f32[2,640,32]{1,2,0:T(8,128)} %param.21) | copy-start | bytes 491524
  97.5 18.5 %copy-start.8 = (f32[2,640,32]{1,2,0:T(8,128)S(1)}, f32[2,640,32]{1,2,0:T(8,128)}, u32[]{:S(2)}) copy-start(f32[2,640,32]{1,2,0:T(8,128)} %param.20) | copy-start | bytes 491524
  116.9 0.7 copy-start.5
  125.4 38.9 %slice-start.2 = ((s8[4423680]{0:T(1024)(128)(4,1)}), s8[4194304]{0:T(1024)(128)(4,1)S(1)}, s32[]{:S(2)}) async-start(s8[4423680]{0:T(1024)(128)(4,1)} %bitcast.115), calls=%async_computation.2 | async-start | bytes 8388608
  128.3 0.8 copy-start.4
  128.3 36.1 %slice-start.3 = ((s8[4423680]{0:T(1024)(128)(4,1)}), s8[229376]{0:T(1024)(128)(4,1)S(1)}, s32[]{:S(2)}) async-start(s8[4423680]{0:T(1024)(128)(4,1)} %bitcast.115), calls=%async_computation.3 | async-start | bytes 458752
